TPU v7x, 32 devices: a whole 2x2x4 slice. The times are simulated.
32 devices in a mesh: blk: 8 (over z, x), red: 4 (over y, core).
Axes of the slice: x: 2, y: 2, z: 4, core: 2. Of those that a mesh axis runs over, the one named last changes fastest.
Arguments:
- resid: float32 [1024, 16384], P('blk', 'red'), may hold values from -64 to 64
- norm_gain: float32 [16384], P('red'), may hold values from 0.1 to 1.9
- w_query: bfloat16 [16384, 16384], P('red', 'blk'), may hold values from -0.046875 to 0.046875
- w_key: bfloat16 [16384, 1024], P('red'), may hold values from -0.046875 to 0.046875
- w_value: bfloat16 [16384, 1024], P('red'), may hold values from -0.046875 to 0.046875
- w_out: bfloat16 [16384, 16384], P('blk', 'red'), may hold values from -0.046875 to 0.046875
- cache_key: bfloat16 [8192, 1024], P('red'), may hold values from -512 to 512
- cache_value: bfloat16 [8192, 1024], P('red'), may hold values from -8 to 8
- prefix_len: int32 [1], replicated, may hold values from 4096 to 8192
Outputs:
- updated: float32 [1024, 16384], P('blk', 'red')
Inputs may be any that keep to these rules, and one draw needn't show every extreme that they name: `prefix_len`: cache slots below it hold the sequence's earlier tokens; the others are unused.
All inputs are finite; a program needn't handle non-finite values.
Results may differ from a plain program's by a relative error of at most 0.003.
The roundings to bfloat16 on the way count: a program that leaves them out, or rounds other values in their place, can miss the bound.
Values may be sent and summed in bfloat16 or wider, within the bound.
No kernel may reach another device: no remote copies, remote signals or barrier semaphores. Data moves between devices by JAX's collectives and lax.ppermute only.
A program may use at most 320 MiB of HBM per device.

v0:
```python
import jax
import jax.numpy as jnp
from jax import lax
from jax.sharding import PartitionSpec as P

KV = 8
HD = 128


theta = 500000.0


def rotate(values, positions):
    half = values.shape[-1] // 2
    steps = jnp.arange(half, dtype=jnp.float32)
    freq = theta ** (-(steps * 2.0) / values.shape[-1])
    angle = positions.astype(jnp.float32)[:, None] * freq[None, :]
    cosine = jnp.cos(angle)[:, None, :]
    sine = jnp.sin(angle)[:, None, :]
    first = values[..., :half]
    second = values[..., half:]
    return jnp.concatenate(
        [first * cosine - second * sine, second * cosine + first * sine], axis=-1
    )


def finish(summed, positions, q_width):
    count = summed.shape[0]
    heads_here = q_width // HD
    query = rotate(summed[:, :q_width].reshape(count, heads_here, HD), positions).astype(
        jnp.bfloat16
    )
    key_new = (
        rotate(summed[:, q_width : q_width + HD].reshape(count, 1, HD), positions)
        .astype(jnp.bfloat16)
        .reshape(count, HD)
    )
    value_new = summed[:, q_width + HD :].astype(jnp.bfloat16)
    return (query, key_new, value_new)


def on_device(resid, norm_gain, w_query, w_key, w_value, w_out, cache_key, cache_value, prefix_len):
    blk_count = lax.axis_size("blk")
    red_count = lax.axis_size("red")
    blk_at = lax.axis_index("blk")
    red_at = lax.axis_index("red")
    total_sq = lax.psum(jnp.sum(resid * resid, axis=1), "red")
    features = resid.shape[1] * red_count
    normed = (resid * lax.rsqrt(total_sq[:, None] / features + 1e-05) * norm_gain[None, :]).astype(
        jnp.bfloat16
    )
    per_head = blk_count // KV
    head_at = blk_at // per_head
    my_wk = lax.dynamic_slice_in_dim(w_key, head_at * HD, HD, 1)
    my_wv = lax.dynamic_slice_in_dim(w_value, head_at * HD, HD, 1)
    joined = jnp.concatenate([w_query, my_wk, my_wv], axis=1)
    partial_proj = jnp.dot(
        lax.all_gather(normed, "blk", axis=0, tiled=True),
        joined,
        preferred_element_type=jnp.float32,
    )
    span = partial_proj.shape[0]
    rows = span // red_count
    q_width = w_query.shape[1]
    start = prefix_len[0]
    low = red_at * rows
    mine = lax.psum_scatter(partial_proj, "red", scatter_dimension=0, tiled=True)
    query, key_new, value_new = finish(
        mine, start + low + jnp.arange(rows, dtype=jnp.int32), q_width
    )
    my_ck = lax.dynamic_slice_in_dim(cache_key, head_at * HD, HD, 1)
    my_cv = lax.dynamic_slice_in_dim(cache_value, head_at * HD, HD, 1)
    c_rows = my_ck.shape[0]
    scale = HD ** (-0.5)
    every = jnp.arange(span, dtype=jnp.int32)
    fresh_k, fresh_v = (
        lax.all_gather(key_new, "red", axis=0, tiled=True),
        lax.all_gather(value_new, "red", axis=0, tiled=True),
    )
    all_ck, all_cv = (
        lax.all_gather(my_ck, "red", axis=0, tiled=True),
        lax.all_gather(my_cv, "red", axis=0, tiled=True),
    )
    cache_ok = (jnp.arange(c_rows * red_count, dtype=jnp.int32) < start)[None, None, :]
    here = low + jnp.arange(rows, dtype=jnp.int32)
    causal = (every[None, :] <= here[:, None])[:, None, :]
    old_scores = (
        jnp.einsum("tgd,cd->tgc", query, all_ck, preferred_element_type=jnp.float32) * scale
    )
    new_scores = (
        jnp.einsum("tgd,sd->tgs", query, fresh_k, preferred_element_type=jnp.float32) * scale
    )
    peak = jnp.maximum(
        jnp.max(jnp.where(cache_ok, old_scores, -1e30), axis=2),
        jnp.max(jnp.where(causal, new_scores, -1e30), axis=2),
    )
    old_w = jnp.where(cache_ok, jnp.exp(old_scores - peak[:, :, None]), 0.0).astype(jnp.bfloat16)
    new_w = jnp.where(causal, jnp.exp(new_scores - peak[:, :, None]), 0.0).astype(jnp.bfloat16)
    total = jnp.sum(old_w, axis=2, dtype=jnp.float32) + jnp.sum(new_w, axis=2, dtype=jnp.float32)
    mixed = jnp.einsum("tgc,cd->tgd", old_w, all_cv, preferred_element_type=jnp.float32)
    mixed = mixed + jnp.einsum("tgs,sd->tgd", new_w, fresh_v, preferred_element_type=jnp.float32)
    attention = (mixed / total[:, :, None]).astype(jnp.bfloat16).reshape(rows, q_width)
    out_terms = jnp.dot(
        lax.all_gather(attention, "red", axis=0, tiled=True),
        w_out,
        preferred_element_type=jnp.float32,
    )
    summed = lax.psum_scatter(out_terms, "blk", scatter_dimension=0, tiled=True)
    return resid + summed


def solution(mesh):
    placed = (
        P("blk", "red"),
        P("red"),
        P("red", "blk"),
        P("red", None),
        P("red", None),
        P("blk", "red"),
        P("red", None),
        P("red", None),
        P(),
    )
    return jax.shard_map(
        on_device, mesh=mesh, in_specs=placed, out_specs=P("blk", "red"), check_vma=False
    )
```

profile of v0, /device:TPU:0, one launch (start us, length us, event | category | flops | bytes accessed | tf_op | source)
XLA Modules:
  0.0 780.2 jit_solution(5740188547134715951)
XLA Ops:
  6.5 0.0 all-gather.5.cloned.1.call-start
  6.5 1.8 multiply_reduce_fusion
  8.4 8.4 %psum.7 = f32[128]{0:T(128)S(1)} all-reduce(f32[128]{0:T(128)S(1)} %multiply_reduce_fusion), channel_id=1, replica_groups=mesh['blk'=8,'red'=4] {'red'}, use_global_device_ids=true, to_apply=%region_1.0 | all-reduce | flops 128 | bytes 1024 | tf_op jit(solution)/shard_map/psum | solution.py:47
  16.7 2.8 multiply_convert_fusion
  19.6 0.0 all-gather.5.cloned.1.call-update
  19.6 0.0 reduce-scatter.3.cloned.1.call-start
  19.7 1.7 constant_dynamic-slice_fusion.2
  21.4 123.6 %all-gather.5.cloned.1.call-done = bf16[1024,4096]{1,0:T(8,128)(2,1)} async-done(((bf16[128,4096]{1,0:T(8,128)(2,1)}), bf16[1024,4096]{1,0:T(8,128)(2,1)}) %all-gather.5.cloned.1.call-update) | async-done | bytes 8388624 | tf_op jit(solution)/shard_map/all_gather | solution.py:58
  145.0 27.2 %fusion = f32[1024,2304]{1,0:T(8,128)} fusion(bf16[1024,4096]{1,0:T(8,128)(2,1)} %all-gather.5.cloned.1.call-done, bf16[4096,128]{1,0:T(8,128)(2,1)S(1)} %get-tuple-element.17, bf16[4096,128]{1,0:T(8,128)(2,1)S(1)} %get-tuple-element.18, bf16[4096,2048]{1,0:T(8,128)(2,1)} %param.11), kind=kOutput, calls=%fused_computation.3 | convolution fusion | flops 19383975936 | bytes 36700160 | tf_op jit(solution)/shard_map/dot_general | solution.py:57
  172.2 0.0 reduce-scatter.3.cloned.1.call-update
  172.2 0.0 all-gather.7.cloned.1.call-start
  172.3 1.9 constant_dynamic-slice_fusion.1
  174.2 0.0 all-gather.7.cloned.1.call-update
  174.2 0.0 all-gather.9.cloned.1.call-start
  174.2 1.1 constant_dynamic-slice_fusion
  175.3 1.0 copy.18
  176.3 0.0 all-gather.9.cloned.1.call-update
  176.3 0.0 all-gather.11.cloned.1.call-start
  177.1 0.2 iota_compare_fusion
  177.3 0.5 multiply_cosine_fusion.1
  177.9 71.1 %reduce-scatter.3.cloned.1.call-done = f32[256,2304]{1,0:T(8,128)} async-done(((f32[1024,2304]{1,0:T(8,128)}), f32[256,2304]{1,0:T(8,128)}) %reduce-scatter.3.cloned.1.call-update) | async-done | bytes 2359312 | tf_op jit(solution)/shard_map/reduce_scatter | solution.py:67
  249.0 1.7 slice_bitcast_fusion
  250.7 0.4 copy.19
  251.1 0.7 fusion.30
  251.8 0.9 slice_bitcast_fusion.1
  252.7 0.6 fusion.22
  253.3 0.1 pad_maximum_fusion.3
  253.4 6.0 all_gather.20
  259.4 1.4 subtract_convert_fusion
  260.7 7.6 select_reduce_fusion.1
  268.3 4.9 all-gather.7.cloned.1.call-done
  273.2 46.1 %select_reduce_fusion = (f32[256,16]{0,1:T(8,128)S(1)}, f32[256,16,8192]{2,0,1:T(8,128)}) fusion(pred[8192]{0:T(1024)(128)(4,1)S(1)} %iota_compare_fusion.1, bf16[8192,128]{1,0:T(8,128)(2,1)} %all-gather.7.cloned.1.call-done, bf16[256,16,64]{2,0,1:T(8,128)(2,1)S(1)} %get-tuple-element.6, bf16[256,16,64]{2,0,1:T(8,128)(2,1)S(1)} %get-tuple-element.5), kind=kOutput, calls=%fused_computation.2 | convolution fusion | flops 8692690944 | bytes 137388032 | tf_op jit(solution)/shard_map/tgd,cd->tgc/dot_general | solution.py:88
  319.3 41.3 %convert_reduce_fusion = f32[256,16]{0,1:T(8,128)S(1)} fusion(f32[256,16]{0,1:T(8,128)S(1)} %max.7, f32[256,16,8192]{2,0,1:T(8,128)} %get-tuple-element.14, pred[8192]{0:T(1024)(128)(4,1)S(1)} %iota_compare_fusion.1), kind=kLoop, calls=%fused_computation | loop fusion | flops 201322496 | bytes 134258688 | tf_op jit(solution)/shard_map/reduce_sum | solution.py:99
  360.6 8.2 %convert_reduce_fusion.1 = f32[256,16]{0,1:T(8,128)S(1)} fusion(f32[256,16]{0,1:T(8,128)S(1)} %max.7, f32[256,16,1024]{2,0,1:T(8,128)} %get-tuple-element.16, pred[256,1024]{1,0:T(8,128)(4,1)S(1)} %iota_compare_fusion), kind=kLoop, calls=%fused_computation.9 | loop fusion | flops 25161728 | bytes 17072128 | tf_op jit(solution)/shard_map/reduce_sum | solution.py:99
  368.8 0.9 slice.51
  369.7 6.0 all_gather.22
  375.7 0.0 all-gather.9.cloned.1.call-done
  375.7 44.1 %fusion.6 = f32[256,16,128]{0,2,1:T(8,128)S(1)} fusion(bf16[8192,128]{0,1:T(8,128)(2,1)} %all-gather.9.cloned.1.call-done, f32[256,16,8192]{2,0,1:T(8,128)} %get-tuple-element.14, f32[256,16]{0,1:T(8,128)S(1)} %max.7, pred[8192]{0:T(1024)(128)(4,1)S(1)} %iota_compare_fusion.1), kind=kOutput, calls=%fused_computation.13 | convolution fusion | flops 8724152320 | bytes 138436608 | tf_op jit(solution)/shard_map/tgc,cd->tgd/dot_general | solution.py:100
  419.9 8.4 %divide_convert_fusion = bf16[256,16,128]{0,2,1:T(8,128)(2,1)} fusion(f32[256,16,128]{0,2,1:T(8,128)S(1)} %fusion.6, f32[256,16]{0,1:T(8,128)S(1)} %add.73, bf16[1024,128]{1,0:T(8,128)(2,1)S(1)} %all_gather.22, f32[256,16,1024]{2,0,1:T(8,128)} %get-tuple-element.16, f32[256,16]{0,1:T(8,128)S(1)} %max.7, pred[256,1024]{1,0:T(8,128)(4,1)S(1)} %iota_compare_fusion), kind=kOutput, calls=%fused_computation.17 | convolution fusion | flops 1092091904 | bytes 20480000 | tf_op jit(solution)/shard_map/tgs,sd->tgd/dot_general | solution.py:101
  428.3 0.0 all-gather.11.cloned.1.call-update
  428.3 0.0 reduce-scatter.5.cloned.1.call-start
  428.4 35.2 %all-gather.11.cloned.1.call-done = bf16[1024,2048]{0,1:T(8,128)(2,1)} async-done(((bf16[256,2048]{0,1:T(8,128)(2,1)}), bf16[1024,2048]{0,1:T(8,128)(2,1)}) %all-gather.11.cloned.1.call-update) | async-done | bytes 4194320 | tf_op jit(solution)/shard_map/all_gather | solution.py:104
  463.5 23.8 %fusion.31 = f32[1024,4096]{1,0:T(8,128)} fusion(bf16[1024,2048]{0,1:T(8,128)(2,1)} %all-gather.11.cloned.1.call-done, bf16[2048,4096]{1,0:T(8,128)(2,1)} %param.14), kind=kOutput, calls=%fused_computation.61 | convolution fusion | flops 17179869184 | bytes 37748736 | tf_op jit(solution)/shard_map/dot_general | solution.py:103
  487.3 0.0 copy-start
  487.3 0.0 reduce-scatter.5.cloned.1.call-update
  487.4 282.9 %reduce-scatter.5.cloned.1.call-done = f32[128,4096]{1,0:T(8,128)} async-done(((f32[1024,4096]{1,0:T(8,128)}), f32[128,4096]{1,0:T(8,128)}) %reduce-scatter.5.cloned.1.call-update) | async-done | bytes 2097168 | tf_op jit(solution)/shard_map/reduce_scatter | solution.py:108
  770.2 0.0 copy-done
  770.2 3.1 add.74
  (7 shorter events, 0.0 us)
Async XLA Ops:
  6.5 138.4 %all-gather.5.cloned.1.call-start = ((), (), s32[]{:S(2)}) async-start(), calls=%async_computation.2 | async-start | bytes 9437184 | tf_op jit(solution)/shard_map/all_gather | solution.py:58
  19.6 229.4 %reduce-scatter.3.cloned.1.call-start = ((), (), s32[]{:S(2)}) async-start(), calls=%async_computation.3 | async-start | bytes 11796480 | tf_op jit(solution)/shard_map/reduce_scatter | solution.py:67
  172.2 100.9 %all-gather.7.cloned.1.call-start = ((), (), s32[]{:S(2)}) async-start(), calls=%async_computation.4 | async-start | bytes 2621440 | tf_op jit(solution)/shard_map/all_gather | solution.py:81
  174.2 201.6 %all-gather.9.cloned.1.call-start = ((), (), s32[]{:S(2)}) async-start(), calls=%async_computation.5 | async-start | bytes 2621440 | tf_op jit(solution)/shard_map/all_gather | solution.py:82
  176.3 287.2 %all-gather.11.cloned.1.call-start = ((), (), s32[]{:S(2)}) async-start(), calls=%async_computation.6 | async-start | bytes 5242880 | tf_op jit(solution)/shard_map/all_gather | solution.py:104
  428.3 341.9 %reduce-scatter.5.cloned.1.call-start = ((), (), s32[]{:S(2)}) async-start(), calls=%async_computation.7 | async-start | bytes 18874368 | tf_op jit(solution)/shard_map/reduce_scatter | solution.py:108
  487.3 282.9 %copy-start = (f32[128,4096]{1,0:T(8,128)S(1)}, f32[128,4096]{1,0:T(8,128)}, u32[]{:S(2)}) copy-start(f32[128,4096]{1,0:T(8,128)} %param.9) | copy-start | bytes 6291460
Sparse Core Ops, SparseCore 0:
  19.7 125.2 all-gather.4
  172.3 76.5 reduce-scatter.2
  250.6 22.5 all-gather.6
  274.6 22.5 all-gather.8
  428.4 35.0 all-gather.10
  487.5 282.7 reduce-scatter.4
where the time goes:
time: 781 us; the launch traced here: 780 us
  waiting for transfers between devices  518 us (66%)
  matrix products  157 us (20%)
  other arithmetic  60.1 us (8%)
  blocking collectives  20.3 us (3%)
  between operations  14.3 us (2%)
  local copies, waits for them, and re-layouts  10.3 us (1%)
    reduce_scatter x1, waiting for transfers between devices, on_device(): summed = lax.psum_scatter(out_terms, 'blk', scatter_dimension=0, tiled=True)  283 us
    all_gather x1, waiting for transfers between devices, on_device(): lax.all_gather(normed, 'blk', axis=0, tiled=True)  124 us
    reduce_scatter x1, waiting for transfers between devices, on_device(): lax.psum_scatter(partial_proj, 'red', scatter_dimension=0, tiled=True)  71.1 us
    dot_general x1, matrix products, on_device(): jnp.einsum('tgd,cd->tgc', query, all_ck, preferred_element_type=jnp.float32)  46.1 us
    dot_general x1, matrix products, on_device(): jnp.einsum('tgc,cd->tgd', old_w, all_cv, preferred_element_type=jnp.float32)  44.1 us
    reduce_sum x1, other arithmetic, on_device(): jnp.sum(old_w, axis=2, dtype=jnp.float32)  41.3 us
    all_gather x1, waiting for transfers between devices, on_device(): lax.all_gather(attention, 'red', axis=0, tiled=True)  35.2 us
    dot_general x1, matrix products, on_device(): jnp.dot(lax.all_gather(normed, 'blk', axis=0, tiled=True), joined, prefer...  27.2 us
  transfers between devices with their start and end apart: 6, of which 5 were waited for; matrix products, arithmetic and copies ran while one was open for 15% of the time, Pallas kernels for 0%

commit v1 on v0

v1 whole, which is shorter than its diff:
```python
import functools
import math

import jax
import jax.numpy as jnp
from jax import lax
from jax.experimental import pallas as pl
from jax.experimental.pallas import tpu as pltpu
from jax.sharding import PartitionSpec as P

KV = 8
HD = 128
THETA = 500000.0
LOW = -1e30
RATE = HD**-0.5 / math.log(2.0)
SHRINK = 1.0 / 32.0
VMEM = 40 * 1024 * 1024


def tables(positions):
    half = HD // 2
    steps = jnp.arange(half, dtype=jnp.float32)
    freq = THETA ** (-(steps * 2.0) / HD)
    angle = positions.astype(jnp.float32)[..., None] * freq
    cosine, sine = jnp.cos(angle), jnp.sin(angle)
    return (
        jnp.concatenate([cosine, cosine], axis=-1),
        jnp.concatenate([-sine, sine], axis=-1),
    )


def fold(score, values, peak, acc):
    new_peak = jnp.maximum(peak, jnp.max(score, axis=1, keepdims=True))
    weights = jnp.exp2((score - new_peak) * RATE).astype(jnp.bfloat16)
    carry = jnp.exp2((peak - new_peak) * RATE)
    ones = jnp.ones(values.shape, values.dtype)
    term = jnp.dot(
        weights, jnp.concatenate([values, ones], axis=1), preferred_element_type=jnp.float32
    )
    return new_peak, acc * carry + term


def scores(query, keys):
    return lax.dot_general(
        query, keys, (((1,), (1,)), ((), ())), preferred_element_type=jnp.float32
    )


def cached_kernel(block, tile, start_ref, raw_ref, cos_ref, sin_ref, kv_ref, q_ref, peak_ref, acc_ref):
    start = start_ref[0]
    heads = raw_ref.shape[1] // HD
    cosine, sine = cos_ref[...], sin_ref[...]
    rotated = []
    for head in range(heads):
        at = slice(head * HD, (head + 1) * HD)
        raw = raw_ref[:, at]
        rotated.append(raw * cosine + pltpu.roll(raw, HD // 2, 1) * sine)
    q_ref[...] = jnp.concatenate(rotated, axis=0).astype(q_ref.dtype)
    peak_ref[...] = jnp.full(peak_ref.shape, LOW, jnp.float32)
    acc_ref[...] = jnp.zeros(acc_ref.shape, jnp.float32)

    def step(index, masked):
        here = pl.ds(pl.multiple_of(index * block, block), block)
        keys, values = kv_ref[here, :HD], kv_ref[here, HD:]
        for low in range(0, q_ref.shape[0], tile):
            rows = slice(low, low + tile)
            score = scores(q_ref[rows, :], keys)
            if masked:
                slot = index * block + lax.broadcasted_iota(jnp.int32, (1, block), 1)
                score = jnp.where(slot < start, score, LOW)
            peak, acc = fold(score, values, peak_ref[rows, :1], acc_ref[rows, :])
            peak_ref[rows, :] = jnp.broadcast_to(peak, (tile, HD))
            acc_ref[rows, :] = acc

    whole = start // block

    @pl.loop(0, whole)
    def _(index):
        step(index, False)

    @pl.when(start > whole * block)
    def _():
        step(whole, True)


def cached_part(start, raw, cosine, sine, cached):
    tokens, width = raw.shape
    rows = tokens * (width // HD)
    slots = cached.shape[0]
    block = min(1024, slots)
    tile = min(512, rows)
    vmem = pl.BlockSpec(memory_space=pltpu.VMEM)
    return pl.pallas_call(
        functools.partial(cached_kernel, block, tile),
        out_shape=(
            jax.ShapeDtypeStruct((rows, HD), jnp.bfloat16),
            jax.ShapeDtypeStruct((rows, HD), jnp.float32),
            jax.ShapeDtypeStruct((rows, 2 * HD), jnp.float32),
        ),
        in_specs=[pl.BlockSpec(memory_space=pltpu.SMEM)] + [vmem] * 4,
        out_specs=(vmem,) * 3,
        compiler_params=pltpu.CompilerParams(vmem_limit_bytes=VMEM),
        cost_estimate=pl.CostEstimate(
            flops=8 * rows * slots * HD,
            bytes_accessed=cached.size * 2 + raw.size * 8,
            transcendentals=rows * slots,
        ),
        name="cached_attention",
    )(start, raw, cosine, sine, cached)


def span_kernel(tile, q_ref, peak_ref, acc_ref, kv_ref, key_at_ref, query_at_ref, out_ref):
    tokens = out_ref.shape[0]
    keys, values = kv_ref[:, :HD], kv_ref[:, HD:]
    key_at = key_at_ref[...]
    for low in range(0, q_ref.shape[0], tile):
        rows = slice(low, low + tile)
        query_at = jnp.concatenate([query_at_ref[...]] * (tile // tokens), axis=0)[:, :1]
        score = jnp.where(key_at <= query_at, scores(q_ref[rows, :], keys), LOW)
        _, acc = fold(score, values, peak_ref[rows, :1], acc_ref[rows, :])
        mixed = (acc[:, :HD] / acc[:, HD:]).astype(out_ref.dtype)
        for part in range(tile // tokens):
            head = low // tokens + part
            out_ref[:, head * HD : (head + 1) * HD] = mixed[part * tokens : (part + 1) * tokens]


def span_part(query, peak, acc, fresh, key_at, query_at):
    tokens = query_at.shape[0]
    rows = query.shape[0]
    vmem = pl.BlockSpec(memory_space=pltpu.VMEM)
    return pl.pallas_call(
        functools.partial(span_kernel, min(512, rows)),
        out_shape=jax.ShapeDtypeStruct((tokens, rows // tokens * HD), jnp.bfloat16),
        in_specs=[vmem] * 6,
        out_specs=vmem,
        compiler_params=pltpu.CompilerParams(vmem_limit_bytes=VMEM),
        cost_estimate=pl.CostEstimate(
            flops=8 * rows * fresh.shape[0] * HD,
            bytes_accessed=rows * HD * 16,
            transcendentals=rows * fresh.shape[0],
        ),
        name="span_attention",
    )(query, peak, acc, fresh, key_at, query_at)


def on_device(resid, norm_gain, w_query, w_key, w_value, w_out, cache_key, cache_value, prefix_len):
    blk_count, red_count = lax.axis_size("blk"), lax.axis_size("red")
    blk_at, red_at = lax.axis_index("blk"), lax.axis_index("red")
    start = prefix_len[0]
    mine, width = resid.shape
    far_count = blk_count // 2
    far_at, near_at = blk_at // 2, blk_at % 2
    bits = [1 << k for k in range(red_count.bit_length() - 1)]

    def swap_red(value, bit):
        return lax.ppermute(value, "red", [(k, k ^ bit) for k in range(red_count)])

    def swap_near(value):
        return lax.ppermute(value, "blk", [(k, k ^ 1) for k in range(blk_count)])

    def move_far(value, pairs):
        pairs = [(2 * a + k, 2 * b + k) for a, b in pairs for k in range(2)]
        return lax.ppermute(value, "blk", pairs)

    line = far_count == 4
    if line:
        at_end = (far_at == 0) | (far_at == 3)
        pairs_out = [(1, 0), (2, 3)]
        pairs_in = [(0, 1), (3, 2)]
        middle = [(1, 2), (2, 1)]
        owners = [
            far_at,
            far_at ^ 1,
            far_at ^ jnp.where(at_end, 2, 3),
            far_at ^ jnp.where(at_end, 3, 2),
        ]
    else:
        owners = [(far_at + j) % far_count for j in range(far_count)]

    def spread(own):
        if line:
            a1 = move_far(own, pairs_out + pairs_in)
            b1 = move_far(own, middle)
            a2 = move_far(b1, pairs_out)
            b2 = move_far(a1, middle)
            a3 = move_far(b2, pairs_out)
            return [own, a1, jnp.where(at_end, a2, b1), jnp.where(at_end, a3, b2)]
        ring = range(far_count)
        return [own] + [
            move_far(own, [((k + j) % far_count, k) for k in ring]) for j in ring if j > 0
        ]

    def collect(parts):
        small = lambda value: value.astype(jnp.float16)
        wide = lambda value: value.astype(jnp.float32)
        if line:
            own, s1, s2, s3 = parts
            a3 = move_far(small(s3), pairs_in)
            a2 = move_far(small(s2), pairs_in)
            b2 = move_far(small(s3 + wide(a3)), middle)
            b1 = move_far(small(s2 + wide(a2)), middle)
            a1 = move_far(small(s1 + wide(b2)), pairs_out + pairs_in)
            return own + wide(a1) + wide(b1)
        total = parts[0]
        ring = range(far_count)
        for j in ring:
            if j > 0:
                moved = move_far(small(parts[j]), [(k, (k + j) % far_count) for k in ring])
                total = total + wide(moved)
        return total

    rows = 2 * mine
    here = rows // red_count
    low = 0
    for k, bit in enumerate(bits):
        low = low + ((red_at // bit) % 2) * (rows >> (k + 1))
    in_block = jnp.arange(mine, dtype=jnp.int32)
    token_at = [
        jnp.concatenate([(owner * 2 + (near_at ^ k)) * mine + in_block for k in range(2)])
        for owner in owners
    ]
    query_at = [lax.dynamic_slice_in_dim(at, low, here) for at in token_at]
    turns = [tables(start + at) for at in query_at]

    def sum_red(value):
        for bit in bits:
            half = value.shape[0] // 2
            side = (red_at // bit) % 2
            keep = lax.dynamic_slice_in_dim(value, side * half, half)
            send = lax.dynamic_slice_in_dim(value, (1 - side) * half, half)
            value = keep + swap_red(send, bit)
        return value

    def join_red(value):
        for bit in reversed(bits):
            got = swap_red(value, bit)
            upper = (red_at // bit) % 2 == 1
            value = jnp.where(
                upper, jnp.concatenate([got, value]), jnp.concatenate([value, got])
            )
        return value

    head_at = blk_at // (blk_count // KV)
    one_head = lambda value: lax.dynamic_slice_in_dim(value, head_at * HD, HD, 1)
    cached = lax.all_gather(
        jnp.concatenate([one_head(cache_key), one_head(cache_value)], axis=1),
        "red",
        axis=0,
        tiled=True,
    )
    w_fresh = jnp.concatenate([one_head(w_key), one_head(w_value)], axis=1)

    total_sq = jnp.sum(resid * resid, axis=1)
    for bit in bits:
        total_sq = total_sq + swap_red(total_sq, bit)
    normed = (
        resid * lax.rsqrt(total_sq[:, None] / (width * red_count) + 1e-05) * norm_gain[None, :]
    ).astype(jnp.bfloat16)

    arrived = [jnp.concatenate([part, swap_near(part)]) for part in spread(normed)]

    def fresh_part(slots):
        raw = [
            jnp.dot(arrived[j], w_fresh, preferred_element_type=jnp.float32) for j in slots
        ]
        summed = sum_red(jnp.concatenate(raw, axis=1)).reshape(here, len(slots), 2, HD)
        key_raw, value = summed[:, :, 0], summed[:, :, 1]
        cosine = jnp.stack([turns[j][0] for j in slots], axis=1)
        sine = jnp.stack([turns[j][1] for j in slots], axis=1)
        key = key_raw * cosine + jnp.roll(key_raw, HD // 2, axis=-1) * sine
        both = jnp.stack([key, value], axis=2).astype(jnp.bfloat16)
        both = join_red(both.reshape(here, len(slots) * 2 * HD))
        return [both[:, k * 2 * HD : (k + 1) * 2 * HD] for k in range(len(slots))]

    slots = range(far_count)
    fresh = fresh_part(slots[:-1]) + fresh_part(slots[-1:])
    fresh = jnp.concatenate(fresh)
    key_at = jnp.concatenate(token_at)[None, :]

    old = []
    for j in slots:
        raw = sum_red(jnp.dot(arrived[j], w_query, preferred_element_type=jnp.float32))
        old.append(cached_part(prefix_len, raw, turns[j][0], turns[j][1], cached))

    parts = [None] * far_count
    for j in reversed(slots):
        at = jnp.broadcast_to(query_at[j][:, None], (here, HD))
        attention = join_red(span_part(*old[j], fresh, key_at, at))
        out = jnp.dot(attention, w_out, preferred_element_type=jnp.float32) * SHRINK
        out = out.astype(jnp.float16)
        got = swap_near(out[mine:])
        parts[j] = out[:mine].astype(jnp.float32) + got.astype(jnp.float32)
    return resid + collect(parts) * (1.0 / SHRINK)


def solution(mesh):
    placed = (
        P("blk", "red"),
        P("red"),
        P("red", "blk"),
        P("red", None),
        P("red", None),
        P("blk", "red"),
        P("red", None),
        P("red", None),
        P(),
    )
    return jax.shard_map(
        on_device, mesh=mesh, in_specs=placed, out_specs=P("blk", "red"), check_vma=False
    )
```

time: 781 us -> 423 us (0.54)
  waiting for transfers between devices: 518 us -> 152 us
  Pallas kernels: 0 us -> 90.5 us
  matrix products: 157 us -> 82.4 us
  starting transfers between devices: 0.21 us -> 46.1 us
  other arithmetic: 60.1 us -> 18.3 us
  blocking collectives: 20.3 us -> 0 us
    reduce_scatter x2 -> x0, waiting for transfers between devices: 354 us -> none  [the longest x1 283 us: on_device(): summed = lax.psum_scatter(out_terms, 'blk', scatter_dimension=0, tiled=True)]
    all_gather x4 -> x1, waiting for transfers between devices: 164 us -> 0.02 us  [on_device(): lax.all_gather(jnp.concatenate([one_head(cache_key), one_head(cache_value...]
    ppermute x0 -> x44, waiting for transfers between devices: none -> 152 us  [the longest x26 59.2 us: swap_red(): return lax.ppermute(value, 'red', [(k, k ^ bit) for k in range(red_count)])]
    pallas_call x0 -> x8, Pallas kernels: none -> 90.5 us  [the longest x4 80.3 us: cached_part(): pl.pallas_call(functools.partial(cached_kernel, block, tile), out_shape=(...]
    dot_general x6 -> x12, matrix products: 157 us -> 82.4 us  [the longest x4 45.4 us: on_device(): out = jnp.dot(attention, w_out, preferred_element_type=jnp.float32) * SHRINK]
    reduce_sum x3 -> x1, other arithmetic: 51.3 us -> 1.82 us  [on_device(): total_sq = jnp.sum(resid * resid, axis=1)]
    ppermute x0 -> x44, starting transfers between devices: none -> 46.1 us  [the longest x10 18.5 us: move_far(): return lax.ppermute(value, 'blk', pairs)]
    all_gather x2 -> x0, blocking collectives: 12 us -> none  [the longest x1 5.99 us: on_device(): lax.all_gather(value_new, 'red', axis=0, tiled=True)]
  transfers between devices with their start and end apart: 6 -> 45, of which waited for: 5 -> 21; matrix products, arithmetic and copies ran while one was open for 15% -> 26% of each run, Pallas kernels for 0% -> 16%
where the time goes in v1:
time: 423 us; the launch traced here: 422 us
  waiting for transfers between devices  152 us (36%)
  Pallas kernels  90.5 us (21%)
  matrix products  82.4 us (19%)
  starting transfers between devices  46.1 us (11%)
  other arithmetic  18.3 us (4%)
  local copies, waits for them, and re-layouts  16.4 us (4%)
  between operations  15.7 us (4%)
    pallas_call x4, Pallas kernels, cached_part(): pl.pallas_call(functools.partial(cached_kernel, block, tile), out_shape=(...  80.3 us
    ppermute x26, waiting for transfers between devices, swap_red(): return lax.ppermute(value, 'red', [(k, k ^ bit) for k in range(red_count)])  59.2 us
    ppermute x8, waiting for transfers between devices, swap_near(): return lax.ppermute(value, 'blk', [(k, k ^ 1) for k in range(blk_count)])  52.6 us
    dot_general x4, matrix products, on_device(): out = jnp.dot(attention, w_out, preferred_element_type=jnp.float32) * SHRINK  45.4 us
    ppermute x10, waiting for transfers between devices, move_far(): return lax.ppermute(value, 'blk', pairs)  40.7 us
    dot_general x4, matrix products, on_device(): jnp.dot(arrived[j], w_query, preferred_element_type=jnp.float32)  31.8 us
    ppermute x10, starting transfers between devices, move_far(): return lax.ppermute(value, 'blk', pairs)  18.5 us
    ppermute x26, starting transfers between devices, swap_red(): return lax.ppermute(value, 'red', [(k, k ^ bit) for k in range(red_count)])  18.4 us
  transfers between devices with their start and end apart: 45, of which 21 were waited for; matrix products, arithmetic and copies ran while one was open for 26% of the time, Pallas kernels for 16%

profile of v1, /device:TPU:0, one launch (start us, length us, event | category | flops | bytes accessed | tf_op | source)
XLA Modules:
  0.0 421.9 jit_solution(15648958925259042281)
XLA Ops:
  6.5 1.8 multiply_reduce_fusion
  8.9 1.3 constant_dynamic-slice_fusion.12
  10.2 1.2 pad_maximum_fusion.10
  14.8 2.6 collective-permute-start.1
  17.4 1.5 collective-permute-done.1
  20.0 2.1 collective-permute-start.2
  23.0 1.8 constant_dynamic-slice_fusion.10
  24.8 4.3 %collective-permute-start.5 = (bf16[128,4096]{1,0:T(8,128)(2,1)S(1)}, bf16[128,4096]{1,0:T(8,128)(2,1)S(1)}, u32[]{:S(2)}, u32[]{:S(2)}) collective-permute-start(bf16[128,4096]{1,0:T(8,128)(2,1)S(1)} %multiply_convert_fusion), channel_id=1, source_target_pairs={{8,0},{12,4},{16,24},{20,28},{0,8},{4,12},{24,16},{28,20},{9,1},{1... | collective-permute-start | bytes 3145736 | tf_op jit(solution)/shard_map/ppermute | solution.py:163
  29.1 1.3 collective-permute-start.8
  30.4 14.3 %collective-permute-done.2 = bf16[128,4096]{1,0:T(8,128)(2,1)S(1)} collective-permute-done((bf16[128,4096]{1,0:T(8,128)(2,1)S(1)}, bf16[128,4096]{1,0:T(8,128)(2,1)S(1)}, u32[]{:S(2)}, u32[]{:S(2)}) %collective-permute-start.2) | collective-permute-done | bytes 1048608 | tf_op jit(solution)/shard_map/ppermute | solution.py:159
  44.7 8.2 %fusion.11 = f32[256,2048]{1,0:T(8,128)S(1)} fusion(bf16[4096,2048]{1,0:T(8,128)(2,1)} %param.11, bf16[128,4096]{1,0:T(8,128)(2,1)S(1)} %collective-permute-done.2, bf16[128,4096]{1,0:T(8,128)(2,1)S(1)} %multiply_convert_fusion), kind=kOutput, calls=%fused_computation.27 | convolution fusion | flops 4299161600 | bytes 20971520 | tf_op jit(solution)/shard_map/dot_general | solution.py:282
  53.9 1.7 collective-permute-start.6
  55.7 1.0 fusion.10
  56.7 17.0 %collective-permute-done.8 = bf16[128,4096]{1,0:T(8,128)(2,1)S(1)} collective-permute-done((bf16[128,4096]{1,0:T(8,128)(2,1)S(1)}, bf16[128,4096]{1,0:T(8,128)(2,1)S(1)}, u32[]{:S(2)}, u32[]{:S(2)}) %collective-permute-start.8) | collective-permute-done | bytes 1048608 | tf_op jit(solution)/shard_map/ppermute | solution.py:163
  74.5 1.3 collective-permute-start.15
  75.8 4.2 collective-permute-done.6
  80.1 8.4 %fusion.62 = f32[256,2048]{1,0:T(8,128)S(1)} fusion(bf16[256,4096]{1,0:T(8,128)(2,1)S(1)} %constant_dynamic-update-slice_fusion, bf16[4096,2048]{1,0:T(8,128)(2,1)} %param.11), kind=kOutput, calls=%fused_computation.181 | convolution fusion | flops 4294967296 | bytes 20971520 | tf_op jit(solution)/shard_map/dot_general | solution.py:282
  88.7 1.7 collective-permute-start.4
  91.6 10.2 %collective-permute-done.4 = f32[64,2048]{1,0:T(8,128)S(1)} collective-permute-done((f32[64,2048]{1,0:T(8,128)S(1)}, f32[64,2048]{1,0:T(8,128)S(1)}, u32[]{:S(2)}, u32[]{:S(2)}) %collective-permute-start.4) | collective-permute-done | bytes 524320 | tf_op jit(solution)/shard_map/ppermute | solution.py:156
  101.8 7.2 %collective-permute-done.15 = bf16[128,4096]{1,0:T(8,128)(2,1)S(1)} collective-permute-done((bf16[128,4096]{1,0:T(8,128)(2,1)S(1)}, bf16[128,4096]{1,0:T(8,128)(2,1)S(1)}, u32[]{:S(2)}, u32[]{:S(2)}) %collective-permute-start.15) | collective-permute-done | bytes 1048608 | tf_op jit(solution)/shard_map/ppermute | solution.py:163
  109.1 1.1 broadcast_select_fusion
  110.2 1.5 collective-permute-start.16
  113.9 1.5 collective-permute-start.25
  116.4 6.0 %fusion.8 = f32[256,2048]{1,0:T(8,128)} fusion(bf16[4096,2048]{1,0:T(8,128)(2,1)S(1)} %bitcast.69, bf16[128,4096]{1,0:T(8,128)(2,1)S(1)} %collective-permute-done.9, bf16[128,4096]{1,0:T(8,128)(2,1)S(1)} %broadcast_select_fusion.1), kind=kOutput, calls=%fused_computation.24 | convolution fusion | flops 4299161600 | bytes 20971520 | tf_op jit(solution)/shard_map/dot_general | solution.py:282
  122.4 14.4 %collective-permute-done.11 = f32[64,768]{0,1:T(8,128)S(1)} collective-permute-done((f32[64,768]{0,1:T(8,128)S(1)}, f32[64,768]{0,1:T(8,128)S(1)}, u32[]{:S(2)}, u32[]{:S(2)}) %collective-permute-start.11) | collective-permute-done | bytes 196640 | tf_op jit(solution)/shard_map/ppermute | solution.py:156
  137.7 1.6 collective-permute-start.12
  139.3 2.4 constant_dynamic-slice_fusion.1
  142.6 2.0 collective-permute-done.13
  145.5 2.3 fusion.7
  148.0 9.2 %fusion.6 = f32[256,2048]{1,0:T(8,128)S(1)} fusion(bf16[4096,2048]{1,0:T(8,128)(2,1)} %param.11, bf16[128,4096]{1,0:T(8,128)(2,1)} %collective-permute-done.16, bf16[128,4096]{1,0:T(8,128)(2,1)} %broadcast_select_fusion), kind=kOutput, calls=%fused_computation.22 | convolution fusion | flops 4299161600 | bytes 20971520 | tf_op jit(solution)/shard_map/dot_general | solution.py:282
  158.5 1.1 constant_dynamic-slice_fusion.3
  159.9 1.7 collective-permute-done.18
  162.3 1.5 reshape.271
  167.6 1.4 dynamic-slice_add_fusion
  169.0 1.7 collective-permute-done.19
  172.1 1.5 dynamic-slice_add_fusion.1
  174.6 11.0 %collective-permute-done.38 = f32[64,2048]{1,0:T(8,128)S(1)} collective-permute-done((f32[64,2048]{1,0:T(8,128)S(1)}, f32[64,2048]{1,0:T(8,128)S(1)}, u32[]{:S(2)}, u32[]{:S(2)}) %collective-permute-start.38) | collective-permute-done | bytes 524320 | tf_op jit(solution)/shard_map/ppermute | solution.py:156
  185.7 10.8 %collective-permute-done.30 = f32[64,2048]{1,0:T(8,128)S(1)} collective-permute-done((f32[64,2048]{1,0:T(8,128)S(1)}, f32[64,2048]{1,0:T(8,128)S(1)}, u32[]{:S(2)}, u32[]{:S(2)}) %collective-permute-start.30) | collective-permute-done | bytes 524320 | tf_op jit(solution)/shard_map/ppermute | solution.py:156
  196.5 2.2 copy-done
  198.7 20.0 %cached_attention.7 = (bf16[1024,128]{1,0:T(8,128)(2,1)S(1)}, f32[1024,128]{1,0:T(8,128)S(1)}, f32[1024,256]{1,0:T(8,128)S(1)}) custom-call(s32[1]{0:T(128)} %copy.45.start_ref, f32[64,2048]{1,0:T(8,128)S(1)} %dynamic-slice_add_fusion.4.raw_ref, f32[64,128]{1,0:T(8,128)S(1)} %get-tuple-element.47.cos_ref, f32[64,128]{1,0:T(8,128)S(1)} %pad_maximum_fusion.19.sin_ref, ...), custom_call_target="tpu_custom_call" | custom-call | flops 8589934592 | bytes 5242880 | tf_op jit(solution)/shard_map/cached_attention/pallas_call | solution.py:93
  218.8 2.5 span_attention.7
  222.2 20.2 %cached_attention.6 = (bf16[1024,128]{1,0:T(8,128)(2,1)S(1)}, f32[1024,128]{1,0:T(8,128)S(1)}, f32[1024,256]{1,0:T(8,128)S(1)}) custom-call(s32[1]{0:T(128)} %copy.45.start_ref, f32[64,2048]{1,0:T(8,128)S(1)} %dynamic-slice_add_fusion.5.raw_ref, f32[64,128]{1,0:T(8,128)S(1)} %pad_maximum_fusion.21.cos_ref, f32[64,128]{1,0:T(8,128)S(1)} %pad_maximum_fusion.22.sin_ref, ...), custom_call_target="tpu_custom_call" | custom-call | flops 8589934592 | bytes 5242880 | tf_op jit(solution)/shard_map/cached_attention/pallas_call | solution.py:93
  242.5 2.5 span_attention.6
  245.0 1.3 collective-permute-start.31
  246.3 20.0 %cached_attention.5 = (bf16[1024,128]{1,0:T(8,128)(2,1)S(1)}, f32[1024,128]{1,0:T(8,128)S(1)}, f32[1024,256]{1,0:T(8,128)S(1)}) custom-call(s32[1]{0:T(128)} %copy.45.start_ref, f32[64,2048]{1,0:T(8,128)S(1)} %dynamic-slice_add_fusion.6.raw_ref, f32[64,128]{1,0:T(8,128)S(1)} %get-tuple-element.44.cos_ref, f32[64,128]{1,0:T(8,128)S(1)} %pad_maximum_fusion.18.sin_ref, ...), custom_call_target="tpu_custom_call" | custom-call | flops 8589934592 | bytes 5242880 | tf_op jit(solution)/shard_map/cached_attention/pallas_call | solution.py:93
  266.3 2.5 span_attention.5
  269.8 20.2 %cached_attention.4 = (bf16[1024,128]{1,0:T(8,128)(2,1)S(1)}, f32[1024,128]{1,0:T(8,128)S(1)}, f32[1024,256]{1,0:T(8,128)S(1)}) custom-call(s32[1]{0:T(128)} %copy.45.start_ref, f32[64,2048]{1,0:T(8,128)S(1)} %dynamic-slice_add_fusion.7.raw_ref, f32[64,128]{1,0:T(8,128)S(1)} %get-tuple-element.42.cos_ref, f32[64,128]{1,0:T(8,128)S(1)} %pad_maximum_fusion.15.sin_ref, ...), custom_call_target="tpu_custom_call" | custom-call | flops 8589934592 | bytes 5242880 | tf_op jit(solution)/shard_map/cached_attention/pallas_call | solution.py:93
  290.0 2.5 span_attention.4
  292.6 1.3 collective-permute-start.21
  294.9 4.8 %collective-permute-done.21 = bf16[64,2048]{1,0:T(8,128)(2,1)S(1)} collective-permute-done((bf16[64,2048]{1,0:T(8,128)(2,1)S(1)}, bf16[64,2048]{1,0:T(8,128)(2,1)S(1)}, u32[]{:S(2)}, u32[]{:S(2)}) %collective-permute-start.21) | collective-permute-done | bytes 262176 | tf_op jit(solution)/shard_map/ppermute | solution.py:156
  299.9 11.4 %fusion.2 = f16[256,4096]{1,0:T(8,128)(2,1)S(1)} fusion(bf16[2048,4096]{1,0:T(8,128)(2,1)} %param.14, bf16[128,2048]{1,0:T(8,128)(2,1)S(1)} %maximum_select_fusion.10, bf16[128,2048]{1,0:T(8,128)(2,1)S(1)} %collective-permute-done.32, pred[]{:T(512)S(6)} %eq.50), kind=kOutput, calls=%fused_computation.6 | convolution fusion | flops 4301783040 | bytes 19922944 | tf_op jit(solution)/shard_map/dot_general | solution.py:289
  312.1 11.3 %fusion.3 = f16[256,4096]{1,0:T(8,128)(2,1)S(1)} fusion(bf16[2048,4096]{1,0:T(8,128)(2,1)} %param.14, bf16[128,2048]{1,0:T(8,128)(2,1)S(1)} %maximum_select_fusion.11, bf16[128,2048]{1,0:T(8,128)(2,1)S(1)} %collective-permute-done.40, pred[]{:T(512)S(6)} %eq.50), kind=kOutput, calls=%fused_computation.7 | convolution fusion | flops 4301783040 | bytes 19922944 | tf_op jit(solution)/shard_map/dot_general | solution.py:289
  323.6 1.5 collective-permute-start.41
  325.2 12.3 %collective-permute-done.33 = f16[128,4096]{1,0:T(8,128)(2,1)S(1)} collective-permute-done((f16[128,4096]{1,0:T(8,128)(2,1)S(1)}, f16[128,4096]{1,0:T(8,128)(2,1)S(1)}, u32[]{:S(2)}, u32[]{:S(2)}) %collective-permute-start.33) | collective-permute-done | bytes 1048608 | tf_op jit(solution)/shard_map/ppermute | solution.py:159
  337.8 1.8 collective-permute-start.34
  339.6 11.4 %fusion.1 = f16[256,4096]{1,0:T(8,128)(2,1)S(1)} fusion(bf16[2048,4096]{1,0:T(8,128)(2,1)} %param.14, bf16[128,2048]{1,0:T(8,128)(2,1)S(1)} %maximum_select_fusion.9, bf16[128,2048]{1,0:T(8,128)(2,1)S(1)} %collective-permute-done.27, pred[]{:T(512)S(6)} %eq.50), kind=kOutput, calls=%fused_computation.5 | convolution fusion | flops 4301783040 | bytes 19922944 | tf_op jit(solution)/shard_map/dot_general | solution.py:289
  351.8 8.2 %collective-permute-done.41 = f16[128,4096]{1,0:T(8,128)(2,1)S(1)} collective-permute-done((f16[128,4096]{1,0:T(8,128)(2,1)S(1)}, f16[128,4096]{1,0:T(8,128)(2,1)S(1)}, u32[]{:S(2)}, u32[]{:S(2)}) %collective-permute-start.41) | collective-permute-done | bytes 1048608 | tf_op jit(solution)/shard_map/ppermute | solution.py:159
  360.3 1.5 collective-permute-start.42
  363.1 11.4 %fusion = f16[256,4096]{1,0:T(8,128)(2,1)S(1)} fusion(bf16[2048,4096]{1,0:T(8,128)(2,1)} %param.14, bf16[128,2048]{1,0:T(8,128)(2,1)S(1)} %maximum_select_fusion.8, bf16[128,2048]{1,0:T(8,128)(2,1)S(1)} %collective-permute-done.22, pred[]{:T(512)S(6)} %eq.50), kind=kOutput, calls=%fused_computation.4 | convolution fusion | flops 4301783040 | bytes 19922944 | tf_op jit(solution)/shard_map/dot_general | solution.py:289
  375.3 8.4 %collective-permute-done.42 = f16[128,4096]{1,0:T(8,128)(2,1)S(1)} collective-permute-done((f16[128,4096]{1,0:T(8,128)(2,1)S(1)}, f16[128,4096]{1,0:T(8,128)(2,1)S(1)}, u32[]{:S(2)}, u32[]{:S(2)}) %collective-permute-start.42) | collective-permute-done | bytes 1048608 | tf_op jit(solution)/shard_map/ppermute | solution.py:163
  385.7 5.3 %collective-permute-start.36 = (f16[128,4096]{1,0:T(8,128)(2,1)S(1)}, f16[128,4096]{1,0:T(8,128)(2,1)S(1)}, u32[]{:S(2)}, u32[]{:S(2)}) collective-permute-start(f16[128,4096]{1,0:T(8,128)(2,1)S(1)} %add_convert_fusion.1), channel_id=1, source_target_pairs={{8,0},{12,4},{16,24},{20,28},{0,8},{4,12},{24,16},{28,20},{9,1},{1... | collective-permute-start | bytes 3145736 | tf_op jit(solution)/shard_map/ppermute | solution.py:163
  391.0 13.5 %collective-permute-done.23 = f16[128,4096]{1,0:T(8,128)(2,1)S(1)} collective-permute-done((f16[128,4096]{1,0:T(8,128)(2,1)S(1)}, f16[128,4096]{1,0:T(8,128)(2,1)S(1)}, u32[]{:S(2)}, u32[]{:S(2)}) %collective-permute-start.23) | collective-permute-done | bytes 1048608 | tf_op jit(solution)/shard_map/ppermute | solution.py:159
  404.5 8.0 %collective-permute-done.36 = f16[128,4096]{1,0:T(8,128)(2,1)S(1)} collective-permute-done((f16[128,4096]{1,0:T(8,128)(2,1)S(1)}, f16[128,4096]{1,0:T(8,128)(2,1)S(1)}, u32[]{:S(2)}, u32[]{:S(2)}) %collective-permute-start.36) | collective-permute-done | bytes 1048608 | tf_op jit(solution)/shard_map/ppermute | solution.py:163
  412.5 2.1 multiply_add_fusion
  (202 shorter events, 32.4 us)
Async XLA Ops:
  6.5 190.0 %all-gather.2.cloned.1.call-start = ((), (), s32[]{:S(2)}) async-start(), calls=%async_computation | async-start | bytes 5242880 | tf_op jit(solution)/shard_map/all_gather | solution.py:245
  8.4 6.4 %collective-permute-start = (f32[128]{0:T(128)S(1)}, f32[128]{0:T(128)S(1)}, u32[]{:S(2)}, u32[]{:S(2)}) collective-permute-start(f32[128]{0:T(128)S(1)} %multiply_reduce_fusion), channel_id=1, source_target_pairs={{0,1},{1,0},{2,3},{3,2},{4,5},{5,4},{6,7},{7,6},{8,9},{9,8},{10,11... | collective-permute-start | bytes 1544 | tf_op jit(solution)/shard_map/ppermute | solution.py:156
  10.2 8.8 %copy-start.2 = (f32[128,4096]{1,0:T(8,128)S(1)}, f32[128,4096]{1,0:T(8,128)}, u32[]{:S(2)}) copy-start(f32[128,4096]{1,0:T(8,128)} %param.9) | copy-start | bytes 6291460
  10.2 8.8 %copy-start.13 = (f32[4096]{0:T(1024)S(1)}, f32[4096]{0:T(1024)}, u32[]{:S(2)}) copy-start(f32[4096]{0:T(1024)} %param.10) | copy-start | bytes 49156
  14.8 4.1 collective-permute-start.1
  19.2 9.9 %collective-permute-start.7 = (bf16[128,4096]{1,0:T(8,128)(2,1)S(1)}, bf16[128,4096]{1,0:T(8,128)(2,1)S(1)}, u32[]{:S(2)}, u32[]{:S(2)}) collective-permute-start(bf16[128,4096]{1,0:T(8,128)(2,1)S(1)} %multiply_convert_fusion), channel_id=1, source_target_pairs={{8,16},{12,20},{16,8},{20,12},{9,17},{13,21},{17,9},{21,13},{10,18... | collective-permute-start | bytes 3145736 | tf_op jit(solution)/shard_map/ppermute | solution.py:163
  20.0 24.7 %collective-permute-start.2 = (bf16[128,4096]{1,0:T(8,128)(2,1)S(1)}, bf16[128,4096]{1,0:T(8,128)(2,1)S(1)}, u32[]{:S(2)}, u32[]{:S(2)}) collective-permute-start(bf16[128,4096]{1,0:T(8,128)(2,1)S(1)} %multiply_convert_fusion), channel_id=1, source_target_pairs={{0,4},{4,0},{8,12},{12,8},{16,20},{20,16},{24,28},{28,24},{1,5},{5... | collective-permute-start | bytes 3145736 | tf_op jit(solution)/shard_map/ppermute | solution.py:159
  24.8 86.9 %copy-start.7 = (bf16[4096,128]{1,0:T(8,128)(2,1)}, bf16[4096,128]{1,0:T(8,128)(2,1)S(1)}, u32[]{:S(2)}) copy-start(bf16[4096,128]{1,0:T(8,128)(2,1)S(1)} %get-tuple-element.77) | copy-start | bytes 3145732
  24.8 86.9 %copy-start.9 = (bf16[4096,128]{1,0:T(8,128)(2,1)}, bf16[4096,128]{1,0:T(8,128)(2,1)S(1)}, u32[]{:S(2)}) copy-start(bf16[4096,128]{1,0:T(8,128)(2,1)S(1)} %get-tuple-element.78) | copy-start | bytes 3145732
  24.8 28.4 %collective-permute-start.5 = (bf16[128,4096]{1,0:T(8,128)(2,1)S(1)}, bf16[128,4096]{1,0:T(8,128)(2,1)S(1)}, u32[]{:S(2)}, u32[]{:S(2)}) collective-permute-start(bf16[128,4096]{1,0:T(8,128)(2,1)S(1)} %multiply_convert_fusion), channel_id=1, source_target_pairs={{8,0},{12,4},{16,24},{20,28},{0,8},{4,12},{24,16},{28,20},{9,1},{1... | collective-permute-start | bytes 3145736 | tf_op jit(solution)/shard_map/ppermute | solution.py:163
  29.1 44.6 %collective-permute-start.8 = (bf16[128,4096]{1,0:T(8,128)(2,1)S(1)}, bf16[128,4096]{1,0:T(8,128)(2,1)S(1)}, u32[]{:S(2)}, u32[]{:S(2)}) collective-permute-start(bf16[128,4096]{1,0:T(8,128)(2,1)S(1)} %collective-permute-done.7), channel_id=1, source_target_pairs={{8,0},{12,4},{16,24},{20,28},{9,1},{13,5},{17,25},{21,29},{10,2},{... | collective-permute-start | bytes 3145736 | tf_op jit(solution)/shard_map/ppermute | solution.py:163
  53.1 35.4 %collective-permute-start.3 = (f32[128,2048]{1,0:T(8,128)S(1)}, f32[128,2048]{1,0:T(8,128)S(1)}, u32[]{:S(2)}, u32[]{:S(2)}) collective-permute-start(f32[128,2048]{1,0:T(8,128)S(1)} %constant_dynamic-slice_fusion.15), channel_id=1, source_target_pairs={{0,1},{1,0},{2,3},{3,2},{4,5},{5,4},{6,7},{7,6},{8,9},{9,8},{10,11... | collective-permute-start | bytes 3145736 | tf_op jit(solution)/shard_map/ppermute | solution.py:156
  53.2 21.3 %collective-permute-start.14 = (bf16[128,4096]{1,0:T(8,128)(2,1)S(1)}, bf16[128,4096]{1,0:T(8,128)(2,1)S(1)}, u32[]{:S(2)}, u32[]{:S(2)}) collective-permute-start(bf16[128,4096]{1,0:T(8,128)(2,1)S(1)} %collective-permute-done.5), channel_id=1, source_target_pairs={{8,16},{12,20},{16,8},{20,12},{9,17},{13,21},{17,9},{21,13},{10,18... | collective-permute-start | bytes 3145736 | tf_op jit(solution)/shard_map/ppermute | solution.py:163
  53.9 26.0 %collective-permute-start.6 = (bf16[128,4096]{1,0:T(8,128)(2,1)S(1)}, bf16[128,4096]{1,0:T(8,128)(2,1)S(1)}, u32[]{:S(2)}, u32[]{:S(2)}) collective-permute-start(bf16[128,4096]{1,0:T(8,128)(2,1)S(1)} %collective-permute-done.5), channel_id=1, source_target_pairs={{0,4},{4,0},{8,12},{12,8},{16,20},{20,16},{24,28},{28,24},{1,5},{5... | collective-permute-start | bytes 3145736 | tf_op jit(solution)/shard_map/ppermute | solution.py:159
  73.8 37.9 %collective-permute-start.9 = (bf16[128,4096]{1,0:T(8,128)(2,1)S(1)}, bf16[128,4096]{1,0:T(8,128)(2,1)S(1)}, u32[]{:S(2)}, u32[]{:S(2)}) collective-permute-start(bf16[128,4096]{1,0:T(8,128)(2,1)S(1)} %broadcast_select_fusion.1), channel_id=1, source_target_pairs={{0,4},{4,0},{8,12},{12,8},{16,20},{20,16},{24,28},{28,24},{1,5},{5... | collective-permute-start | bytes 3145736 | tf_op jit(solution)/shard_map/ppermute | solution.py:159
  74.5 34.6 %collective-permute-start.15 = (bf16[128,4096]{1,0:T(8,128)(2,1)S(1)}, bf16[128,4096]{1,0:T(8,128)(2,1)S(1)}, u32[]{:S(2)}, u32[]{:S(2)}) collective-permute-start(bf16[128,4096]{1,0:T(8,128)(2,1)S(1)} %collective-permute-done.14), channel_id=1, source_target_pairs={{8,0},{12,4},{16,24},{20,28},{9,1},{13,5},{17,25},{21,29},{10,2},{... | collective-permute-start | bytes 3145736 | tf_op jit(solution)/shard_map/ppermute | solution.py:163
  88.5 27.9 %slice-start = ((s8[16777216]{0:T(1024)(128)(4,1)}), s8[4194304]{0:T(1024)(128)(4,1)S(1)}, s32[]{:S(2)}) async-start(s8[16777216]{0:T(1024)(128)(4,1)} %bitcast.68), calls=%async_computation.1 | async-start | bytes 8388608
  88.7 13.1 %collective-permute-start.4 = (f32[64,2048]{1,0:T(8,128)S(1)}, f32[64,2048]{1,0:T(8,128)S(1)}, u32[]{:S(2)}, u32[]{:S(2)}) collective-permute-start(f32[64,2048]{1,0:T(8,128)S(1)} %constant_dynamic-slice_fusion.14), channel_id=1, source_target_pairs={{0,2},{1,3},{2,0},{3,1},{4,6},{5,7},{6,4},{7,5},{8,10},{9,11},{10,... | collective-permute-start | bytes 1572872 | tf_op jit(solution)/shard_map/ppermute | solution.py:156
  90.5 25.9 %slice-start.1 = ((s8[16777216]{0:T(1024)(128)(4,1)}), s8[4194304]{0:T(1024)(128)(4,1)S(1)}, s32[]{:S(2)}) async-start(s8[16777216]{0:T(1024)(128)(4,1)} %bitcast.68), calls=%async_computation.2 | async-start | bytes 8388608
  90.5 22.4 %collective-permute-start.24 = (f32[128,2048]{1,0:T(8,128)S(1)}, f32[128,2048]{1,0:T(8,128)S(1)}, u32[]{:S(2)}, u32[]{:S(2)}) collective-permute-start(f32[128,2048]{1,0:T(8,128)S(1)} %constant_dynamic-slice_fusion.5), channel_id=1, source_target_pairs={{0,1},{1,0},{2,3},{3,2},{4,5},{5,4},{6,7},{7,6},{8,9},{9,8},{10,11... | collective-permute-start | bytes 3145736 | tf_op jit(solution)/shard_map/ppermute | solution.py:156
  101.8 14.6 %slice-start.2 = ((s8[16777216]{0:T(1024)(128)(4,1)}), s8[4194304]{0:T(1024)(128)(4,1)S(1)}, s32[]{:S(2)}) async-start(s8[16777216]{0:T(1024)(128)(4,1)} %bitcast.68), calls=%async_computation.3 | async-start | bytes 8388608
  110.2 35.3 %collective-permute-start.16 = (bf16[128,4096]{1,0:T(8,128)(2,1)}, bf16[128,4096]{1,0:T(8,128)(2,1)}, u32[]{:S(2)}, u32[]{:S(2)}) collective-permute-start(bf16[128,4096]{1,0:T(8,128)(2,1)} %broadcast_select_fusion), channel_id=1, source_target_pairs={{0,4},{4,0},{8,12},{12,8},{16,20},{20,16},{24,28},{28,24},{1,5},{5... | collective-permute-start | bytes 3145736 | tf_op jit(solution)/shard_map/ppermute | solution.py:159
  112.7 3.7 slice-start.3
  112.8 2.6 collective-permute-start.10
  113.9 28.6 %collective-permute-start.25 = (f32[64,2048]{1,0:T(8,128)}, f32[64,2048]{1,0:T(8,128)S(1)}, u32[]{:S(2)}, u32[]{:S(2)}) collective-permute-start(f32[64,2048]{1,0:T(8,128)} %constant_dynamic-slice_fusion.4), channel_id=1, source_target_pairs={{0,2},{1,3},{2,0},{3,1},{4,6},{5,7},{6,4},{7,5},{8,10},{9,11},{10,... | collective-permute-start | bytes 1572872 | tf_op jit(solution)/shard_map/ppermute | solution.py:156
  115.6 21.2 %collective-permute-start.11 = (f32[64,768]{0,1:T(8,128)S(1)}, f32[64,768]{0,1:T(8,128)S(1)}, u32[]{:S(2)}, u32[]{:S(2)}) collective-permute-start(f32[64,768]{0,1:T(8,128)S(1)} %constant_dynamic-slice_fusion.8), channel_id=1, source_target_pairs={{0,2},{1,3},{2,0},{3,1},{4,6},{5,7},{6,4},{7,5},{8,10},{9,11},{10,... | collective-permute-start | bytes 589832 | tf_op jit(solution)/shard_map/ppermute | solution.py:156
  137.7 4.7 %collective-permute-start.12 = (bf16[64,768]{1,0:T(8,128)(2,1)S(1)}, bf16[64,768]{1,0:T(8,128)(2,1)S(1)}, u32[]{:S(2)}, u32[]{:S(2)}) collective-permute-start(bf16[64,768]{1,0:T(8,128)(2,1)S(1)} %convert_element_type.97), channel_id=1, source_target_pairs={{0,2},{1,3},{2,0},{3,1},{4,6},{5,7},{6,4},{7,5},{8,10},{9,11},{10,... | collective-permute-start | bytes 294920 | tf_op jit(solution)/shard_map/ppermute | solution.py:156
  141.7 3.8 copy-start.8
  141.7 3.8 copy-start.10
  141.7 25.9 %collective-permute-start.37 = (f32[128,2048]{1,0:T(8,128)}, f32[128,2048]{1,0:T(8,128)}, u32[]{:S(2)}, u32[]{:S(2)}) collective-permute-start(f32[128,2048]{1,0:T(8,128)} %constant_dynamic-slice_fusion.1), channel_id=1, source_target_pairs={{0,1},{1,0},{2,3},{3,2},{4,5},{5,4},{6,7},{7,6},{8,9},{9,8},{10,11... | collective-permute-start | bytes 3145736 | tf_op jit(solution)/shard_map/ppermute | solution.py:156
  142.4 2.2 collective-permute-start.13
  147.8 9.4 %collective-permute-start.17 = (f32[128,256]{1,0:T(8,128)S(1)}, f32[128,256]{1,0:T(8,128)S(1)}, u32[]{:S(2)}, u32[]{:S(2)}) collective-permute-start(f32[128,256]{1,0:T(8,128)S(1)} %constant_dynamic-slice_fusion.7), channel_id=1, source_target_pairs={{0,1},{1,0},{2,3},{3,2},{4,5},{5,4},{6,7},{7,6},{8,9},{9,8},{10,11... | collective-permute-start | bytes 393224 | tf_op jit(solution)/shard_map/ppermute | solution.py:156
  157.2 1.3 copy-start.5
  157.2 10.4 %copy-start.4 = (f32[256,2048]{1,0:T(8,128)S(1)}, f32[256,2048]{1,0:T(8,128)}, u32[]{:S(2)}) copy-start(f32[256,2048]{1,0:T(8,128)} %fusion.8) | copy-start | bytes 6291460
  157.2 4.4 %collective-permute-start.18 = (f32[64,256]{1,0:T(8,128)S(1)}, f32[64,256]{1,0:T(8,128)S(1)}, u32[]{:S(2)}, u32[]{:S(2)}) collective-permute-start(f32[64,256]{1,0:T(8,128)S(1)} %constant_dynamic-slice_fusion.6), channel_id=1, source_target_pairs={{0,2},{1,3},{2,0},{3,1},{4,6},{5,7},{6,4},{7,5},{8,10},{9,11},{10,... | collective-permute-start | bytes 196616 | tf_op jit(solution)/shard_map/ppermute | solution.py:156
  159.6 12.5 %collective-permute-start.29 = (f32[128,2048]{1,0:T(8,128)}, f32[128,2048]{1,0:T(8,128)}, u32[]{:S(2)}, u32[]{:S(2)}) collective-permute-start(f32[128,2048]{1,0:T(8,128)} %constant_dynamic-slice_fusion.3), channel_id=1, source_target_pairs={{0,1},{1,0},{2,3},{3,2},{4,5},{5,4},{6,7},{7,6},{8,9},{9,8},{10,11... | collective-permute-start | bytes 3145736 | tf_op jit(solution)/shard_map/ppermute | solution.py:156
  166.7 5.4 %copy-start.6 = (f32[256,2048]{1,0:T(8,128)S(1)}, f32[256,2048]{1,0:T(8,128)}, u32[]{:S(2)}) copy-start(f32[256,2048]{1,0:T(8,128)} %copy-done.5) | copy-start | bytes 6291460
  166.7 4.0 collective-permute-start.19
  170.7 1.3 collective-permute-start.20
  170.8 14.8 %collective-permute-start.38 = (f32[64,2048]{1,0:T(8,128)S(1)}, f32[64,2048]{1,0:T(8,128)S(1)}, u32[]{:S(2)}, u32[]{:S(2)}) collective-permute-start(f32[64,2048]{1,0:T(8,128)S(1)} %constant_dynamic-slice_fusion), channel_id=1, source_target_pairs={{0,2},{1,3},{2,0},{3,1},{4,6},{5,7},{6,4},{7,5},{8,10},{9,11},{10,... | collective-permute-start | bytes 1572872 | tf_op jit(solution)/shard_map/ppermute | solution.py:156
  172.0 2.5 copy-start.11
  172.0 2.5 copy-start.12
  173.6 22.8 %collective-permute-start.30 = (f32[64,2048]{1,0:T(8,128)S(1)}, f32[64,2048]{1,0:T(8,128)S(1)}, u32[]{:S(2)}, u32[]{:S(2)}) collective-permute-start(f32[64,2048]{1,0:T(8,128)S(1)} %constant_dynamic-slice_fusion.2), channel_id=1, source_target_pairs={{0,2},{1,3},{2,0},{3,1},{4,6},{5,7},{6,4},{7,5},{8,10},{9,11},{10,... | collective-permute-start | bytes 1572872 | tf_op jit(solution)/shard_map/ppermute | solution.py:156
  196.5 2.2 copy-start
  198.7 20.0 %copy-start.14 = (s32[64]{0:T(128)S(1)}, s32[64]{0:T(128)}, u32[]{:S(2)}) copy-start(s32[64]{0:T(128)} %get-tuple-element.36) | copy-start | bytes 772
  198.7 23.5 %copy-start.1 = (bf16[8192,256]{1,0:T(8,128)(2,1)S(1)}, bf16[8192,256]{1,0:T(8,128)(2,1)}, u32[]{:S(2)}) copy-start(bf16[8192,256]{1,0:T(8,128)(2,1)} %all-gather.2.cloned.1.call-done.kv_ref) | copy-start | bytes 12582916
  221.3 72.7 %collective-permute-start.39 = (bf16[64,2048]{1,0:T(8,128)(2,1)S(1)}, bf16[64,2048]{1,0:T(8,128)(2,1)S(1)}, u32[]{:S(2)}, u32[]{:S(2)}) collective-permute-start(bf16[64,2048]{1,0:T(8,128)(2,1)S(1)} %span_attention.7), channel_id=1, source_target_pairs={{0,2},{1,3},{2,0},{3,1},{4,6},{5,7},{6,4},{7,5},{8,10},{9,11},{10,... | collective-permute-start | bytes 786440 | tf_op jit(solution)/shard_map/ppermute | solution.py:156
  245.0 48.8 %collective-permute-start.31 = (bf16[64,2048]{1,0:T(8,128)(2,1)S(1)}, bf16[64,2048]{1,0:T(8,128)(2,1)S(1)}, u32[]{:S(2)}, u32[]{:S(2)}) collective-permute-start(bf16[64,2048]{1,0:T(8,128)(2,1)S(1)} %span_attention.6), channel_id=1, source_target_pairs={{0,2},{1,3},{2,0},{3,1},{4,6},{5,7},{6,4},{7,5},{8,10},{9,11},{10,... | collective-permute-start | bytes 786440 | tf_op jit(solution)/shard_map/ppermute | solution.py:156
  268.9 25.8 %collective-permute-start.26 = (bf16[64,2048]{1,0:T(8,128)(2,1)S(1)}, bf16[64,2048]{1,0:T(8,128)(2,1)S(1)}, u32[]{:S(2)}, u32[]{:S(2)}) collective-permute-start(bf16[64,2048]{1,0:T(8,128)(2,1)S(1)} %span_attention.5), channel_id=1, source_target_pairs={{0,2},{1,3},{2,0},{3,1},{4,6},{5,7},{6,4},{7,5},{8,10},{9,11},{10,... | collective-permute-start | bytes 786440 | tf_op jit(solution)/shard_map/ppermute | solution.py:156
  292.6 7.1 %collective-permute-start.21 = (bf16[64,2048]{1,0:T(8,128)(2,1)S(1)}, bf16[64,2048]{1,0:T(8,128)(2,1)S(1)}, u32[]{:S(2)}, u32[]{:S(2)}) collective-permute-start(bf16[64,2048]{1,0:T(8,128)(2,1)S(1)} %span_attention.4), channel_id=1, source_target_pairs={{0,2},{1,3},{2,0},{3,1},{4,6},{5,7},{6,4},{7,5},{8,10},{9,11},{10,... | collective-permute-start | bytes 786440 | tf_op jit(solution)/shard_map/ppermute | solution.py:156
  294.0 6.0 %collective-permute-start.32 = (bf16[128,2048]{1,0:T(8,128)(2,1)S(1)}, bf16[128,2048]{1,0:T(8,128)(2,1)S(1)}, u32[]{:S(2)}, u32[]{:S(2)}) collective-permute-start(bf16[128,2048]{1,0:T(8,128)(2,1)S(1)} %maximum_select_fusion.10), channel_id=1, source_target_pairs={{0,1},{1,0},{2,3},{3,2},{4,5},{5,4},{6,7},{7,6},{8,9},{9,8},{10,11... | collective-permute-start | bytes 1572872 | tf_op jit(solution)/shard_map/ppermute | solution.py:156
  294.2 17.9 %collective-permute-start.40 = (bf16[128,2048]{1,0:T(8,128)(2,1)S(1)}, bf16[128,2048]{1,0:T(8,128)(2,1)S(1)}, u32[]{:S(2)}, u32[]{:S(2)}) collective-permute-start(bf16[128,2048]{1,0:T(8,128)(2,1)S(1)} %maximum_select_fusion.11), channel_id=1, source_target_pairs={{0,1},{1,0},{2,3},{3,2},{4,5},{5,4},{6,7},{7,6},{8,9},{9,8},{10,11... | collective-permute-start | bytes 1572872 | tf_op jit(solution)/shard_map/ppermute | solution.py:156
  294.8 44.8 %collective-permute-start.27 = (bf16[128,2048]{1,0:T(8,128)(2,1)S(1)}, bf16[128,2048]{1,0:T(8,128)(2,1)S(1)}, u32[]{:S(2)}, u32[]{:S(2)}) collective-permute-start(bf16[128,2048]{1,0:T(8,128)(2,1)S(1)} %maximum_select_fusion.9), channel_id=1, source_target_pairs={{0,1},{1,0},{2,3},{3,2},{4,5},{5,4},{6,7},{7,6},{8,9},{9,8},{10,11... | collective-permute-start | bytes 1572872 | tf_op jit(solution)/shard_map/ppermute | solution.py:156
  299.8 63.3 %collective-permute-start.22 = (bf16[128,2048]{1,0:T(8,128)(2,1)S(1)}, bf16[128,2048]{1,0:T(8,128)(2,1)S(1)}, u32[]{:S(2)}, u32[]{:S(2)}) collective-permute-start(bf16[128,2048]{1,0:T(8,128)(2,1)S(1)} %maximum_select_fusion.8), channel_id=1, source_target_pairs={{0,1},{1,0},{2,3},{3,2},{4,5},{5,4},{6,7},{7,6},{8,9},{9,8},{10,11... | collective-permute-start | bytes 1572872 | tf_op jit(solution)/shard_map/ppermute | solution.py:156
  311.5 26.0 %collective-permute-start.33 = (f16[128,4096]{1,0:T(8,128)(2,1)S(1)}, f16[128,4096]{1,0:T(8,128)(2,1)S(1)}, u32[]{:S(2)}, u32[]{:S(2)}) collective-permute-start(f16[128,4096]{1,0:T(8,128)(2,1)S(1)} %slice.98), channel_id=1, source_target_pairs={{0,4},{4,0},{8,12},{12,8},{16,20},{20,16},{24,28},{28,24},{1,5},{5... | collective-permute-start | bytes 3145736 | tf_op jit(solution)/shard_map/ppermute | solution.py:159
  323.6 36.3 %collective-permute-start.41 = (f16[128,4096]{1,0:T(8,128)(2,1)S(1)}, f16[128,4096]{1,0:T(8,128)(2,1)S(1)}, u32[]{:S(2)}, u32[]{:S(2)}) collective-permute-start(f16[128,4096]{1,0:T(8,128)(2,1)S(1)} %slice.100), channel_id=1, source_target_pairs={{0,4},{4,0},{8,12},{12,8},{16,20},{20,16},{24,28},{28,24},{1,5},{5... | collective-permute-start | bytes 3145736 | tf_op jit(solution)/shard_map/ppermute | solution.py:159
  337.8 24.0 %collective-permute-start.34 = (f16[128,4096]{1,0:T(8,128)(2,1)S(1)}, f16[128,4096]{1,0:T(8,128)(2,1)S(1)}, u32[]{:S(2)}, u32[]{:S(2)}) collective-permute-start(f16[128,4096]{1,0:T(8,128)(2,1)S(1)} %fusion.4), channel_id=1, source_target_pairs={{0,8},{4,12},{24,16},{28,20},{1,9},{5,13},{25,17},{29,21},{2,10},{... | collective-permute-start | bytes 3145736 | tf_op jit(solution)/shard_map/ppermute | solution.py:163
  351.2 33.9 %collective-permute-start.28 = (f16[128,4096]{1,0:T(8,128)(2,1)S(1)}, f16[128,4096]{1,0:T(8,128)(2,1)S(1)}, u32[]{:S(2)}, u32[]{:S(2)}) collective-permute-start(f16[128,4096]{1,0:T(8,128)(2,1)S(1)} %slice.96), channel_id=1, source_target_pairs={{0,4},{4,0},{8,12},{12,8},{16,20},{20,16},{24,28},{28,24},{1,5},{5... | collective-permute-start | bytes 3145736 | tf_op jit(solution)/shard_map/ppermute | solution.py:159
  360.3 23.4 %collective-permute-start.42 = (f16[128,4096]{1,0:T(8,128)(2,1)S(1)}, f16[128,4096]{1,0:T(8,128)(2,1)S(1)}, u32[]{:S(2)}, u32[]{:S(2)}) collective-permute-start(f16[128,4096]{1,0:T(8,128)(2,1)S(1)} %fusion.5), channel_id=1, source_target_pairs={{0,8},{4,12},{24,16},{28,20},{1,9},{5,13},{25,17},{29,21},{2,10},{... | collective-permute-start | bytes 3145736 | tf_op jit(solution)/shard_map/ppermute | solution.py:163
  362.4 22.8 %collective-permute-start.35 = (f16[128,4096]{1,0:T(8,128)(2,1)S(1)}, f16[128,4096]{1,0:T(8,128)(2,1)S(1)}, u32[]{:S(2)}, u32[]{:S(2)}) collective-permute-start(f16[128,4096]{1,0:T(8,128)(2,1)S(1)} %add_convert_fusion.2), channel_id=1, source_target_pairs={{8,16},{12,20},{16,8},{20,12},{9,17},{13,21},{17,9},{21,13},{10,18... | collective-permute-start | bytes 3145736 | tf_op jit(solution)/shard_map/ppermute | solution.py:163
  374.7 29.8 %collective-permute-start.23 = (f16[128,4096]{1,0:T(8,128)(2,1)S(1)}, f16[128,4096]{1,0:T(8,128)(2,1)S(1)}, u32[]{:S(2)}, u32[]{:S(2)}) collective-permute-start(f16[128,4096]{1,0:T(8,128)(2,1)S(1)} %slice.94), channel_id=1, source_target_pairs={{0,4},{4,0},{8,12},{12,8},{16,20},{20,16},{24,28},{28,24},{1,5},{5... | collective-permute-start | bytes 3145736 | tf_op jit(solution)/shard_map/ppermute | solution.py:159
  384.2 28.2 %copy-start.3 = (f32[128,4096]{1,0:T(8,128)S(1)}, f32[128,4096]{1,0:T(8,128)}, u32[]{:S(2)}) copy-start(f32[128,4096]{1,0:T(8,128)} %param.9) | copy-start | bytes 6291460
  384.2 20.3 %collective-permute-start.43 = (f16[128,4096]{1,0:T(8,128)(2,1)S(1)}, f16[128,4096]{1,0:T(8,128)(2,1)S(1)}, u32[]{:S(2)}, u32[]{:S(2)}) collective-permute-start(f16[128,4096]{1,0:T(8,128)(2,1)S(1)} %add_convert_fusion), channel_id=1, source_target_pairs={{8,16},{12,20},{16,8},{20,12},{9,17},{13,21},{17,9},{21,13},{10,18... | collective-permute-start | bytes 3145736 | tf_op jit(solution)/shard_map/ppermute | solution.py:163
  385.7 26.8 %collective-permute-start.36 = (f16[128,4096]{1,0:T(8,128)(2,1)S(1)}, f16[128,4096]{1,0:T(8,128)(2,1)S(1)}, u32[]{:S(2)}, u32[]{:S(2)}) collective-permute-start(f16[128,4096]{1,0:T(8,128)(2,1)S(1)} %add_convert_fusion.1), channel_id=1, source_target_pairs={{8,0},{12,4},{16,24},{20,28},{0,8},{4,12},{24,16},{28,20},{9,1},{1... | collective-permute-start | bytes 3145736 | tf_op jit(solution)/shard_map/ppermute | solution.py:163
Sparse Core Ops, SparseCore 0:
  11.5 36.8 all-gather.1

commit v2 on v0

v2 whole, which is shorter than its diff:
```python
import functools
import math

import jax
import jax.numpy as jnp
from jax import lax
from jax.experimental import pallas as pl
from jax.experimental.pallas import tpu as pltpu
from jax.sharding import PartitionSpec as P

KV = 8
HD = 128
THETA = 500000.0
LOW = -1e30
RATE = HD**-0.5 / math.log(2.0)
SHRINK = 1.0 / 32.0
MIB = 1024 * 1024
PIECES = 2
COST = pl.CostEstimate(flops=0, bytes_accessed=0, transcendentals=0)


def tables(positions):
    half = HD // 2
    steps = jnp.arange(half, dtype=jnp.float32)
    freq = THETA ** (-(steps * 2.0) / HD)
    angle = positions.astype(jnp.float32)[..., None] * freq
    cosine, sine = jnp.cos(angle), jnp.sin(angle)
    return (
        jnp.concatenate([cosine, cosine], axis=-1),
        jnp.concatenate([-sine, sine], axis=-1),
    )


def fold(parts, peak, acc):
    lanes = [score[:, at : at + HD] for score, _ in parts for at in range(0, score.shape[1], HD)]
    top = jnp.max(functools.reduce(jnp.maximum, lanes), axis=1, keepdims=True)
    new_peak = jnp.maximum(peak, top)
    carry = jnp.exp2((peak - new_peak) * RATE)
    acc = acc * jnp.concatenate([carry, carry], axis=1)
    for score, values in parts:
        shift = jnp.concatenate([new_peak] * (score.shape[1] // HD), axis=1)
        weights = jnp.exp2((score - shift) * RATE).astype(jnp.bfloat16)
        both = jnp.concatenate([values, jnp.ones(values.shape, values.dtype)], axis=1)
        acc = acc + jnp.dot(weights, both, preferred_element_type=jnp.float32)
    return new_peak, acc


def scores(query, keys):
    return lax.dot_general(
        query, keys, (((1,), (1,)), ((), ())), preferred_element_type=jnp.float32
    )


def attention_kernel(base_at, far_count, slot, unit, tile, cached, spanned, *refs):
    refs = list(refs)
    facts_ref = refs.pop(0)
    if cached:
        keep_ref, got_ref, cos_ref, sin_ref, key_ref, value_ref = refs[:6]
        refs = refs[6:]
    else:
        old_q_ref, old_peak_ref, old_acc_ref = refs[:3]
        refs = refs[3:]
    if spanned:
        fresh_ref, out_ref = refs[:2]
        refs = refs[2:]
    q_ref, peak_ref, acc_ref = refs if cached else (old_q_ref, old_peak_ref, old_acc_ref)
    start = facts_ref[0]
    rows_here = q_ref.shape[0]
    tiles = [slice(low, low + tile) for low in range(0, rows_here, tile)]

    def step(base, count, masked):
        for rows in tiles:
            parts = []
            for k in range(count):
                low = pl.multiple_of(base + k * unit, unit)
                here = pl.ds(low, unit)
                score = jnp.dot(
                    q_ref[rows, :], key_ref[:, here], preferred_element_type=jnp.float32
                )
                if masked and k == count - 1:
                    at = low + lax.broadcasted_iota(jnp.int32, (1, unit), 1)
                    score = jnp.where(at < start, score, LOW)
                parts.append((score, value_ref[here, :]))
            peak_ref[rows, :], acc_ref[rows, :] = fold(parts, peak_ref[rows, :], acc_ref[rows, :])

    if cached:
        tokens = keep_ref.shape[0]
        mine = slice(slot * tokens, (slot + 1) * tokens)
        cosine, sine = cos_ref[mine, :], sin_ref[mine, :]
        rotated = []
        for head in range(keep_ref.shape[1] // HD):
            at = slice(head * HD, (head + 1) * HD)
            raw = keep_ref[:, at] + got_ref[:, at]
            rotated.append(raw * cosine + pltpu.roll(raw, HD // 2, 1) * sine)
        q_ref[...] = jnp.concatenate(rotated, axis=0).astype(q_ref.dtype)
        peak_ref[...] = jnp.full(peak_ref.shape, LOW, jnp.float32)
        acc_ref[...] = jnp.zeros(acc_ref.shape, jnp.float32)
        pairs = start // (2 * unit)
        done = pairs * (2 * unit)

        @pl.loop(0, pairs)
        def _(index):
            step(index * (2 * unit), 2, False)

        @pl.when((start > done) & (start <= done + unit))
        def _():
            step(done, 1, True)

        @pl.when(start > done + unit)
        def _():
            step(done, 2, True)

    if spanned:
        tokens = out_ref.shape[0]
        keys, values = fresh_ref[:, :HD], fresh_ref[:, HD:]
        far, near = facts_ref[base_at - 2], facts_ref[base_at - 1]
        own = fresh_ref.shape[0] // (2 * far_count)
        in_block = lax.broadcasted_iota(jnp.int32, (1, own), 1)
        key_at = jnp.concatenate(
            [
                in_block + ((far ^ d) * 2 + (near ^ k)) * own
                for d in range(far_count)
                for k in range(2)
            ],
            axis=1,
        )
        query_at = facts_ref[base_at + slot] + lax.broadcasted_iota(jnp.int32, (tokens, 1), 0)
        query_at = jnp.concatenate([query_at] * (tile // tokens), axis=0)
        for rows in tiles:
            score = jnp.where(key_at <= query_at, scores(q_ref[rows, :], keys), LOW)
            _, acc = fold([(score, values)], peak_ref[rows, :], acc_ref[rows, :])
            mixed = (acc[:, :HD] / acc[:, HD:]).astype(out_ref.dtype)
            for part in range(tile // tokens):
                head = rows.start // tokens + part
                out_ref[:, head * HD : (head + 1) * HD] = mixed[
                    part * tokens : (part + 1) * tokens
                ]


def attend(base_at, far_count, slot, facts, tokens, rows, old, new):
    cached = len(old) == 6
    spanned = new is not None
    unit = min(1024, old[5].shape[0] // 2) if cached else 0
    tile = min(256, rows)
    vmem = pl.BlockSpec(memory_space=pltpu.VMEM)
    state = [
        ((rows, HD), jnp.bfloat16),
        ((rows, HD), jnp.float32),
        ((rows, 2 * HD), jnp.float32),
    ]
    if spanned:
        out_shape = jax.ShapeDtypeStruct((tokens, rows // tokens * HD), jnp.bfloat16)
    else:
        out_shape = tuple(jax.ShapeDtypeStruct(*one) for one in state)
    operands = [*old, *([new] if spanned else [])]
    return pl.pallas_call(
        functools.partial(attention_kernel, base_at, far_count, slot, unit, tile, cached, spanned),
        out_shape=out_shape,
        in_specs=[pl.BlockSpec(memory_space=pltpu.SMEM)] + [vmem] * len(operands),
        out_specs=vmem if spanned else (vmem,) * 3,
        scratch_shapes=[pltpu.VMEM(*one) for one in state] if cached and spanned else [],
        compiler_params=pltpu.CompilerParams(vmem_limit_bytes=(9 if cached else 5) * MIB),
        cost_estimate=pl.CostEstimate(
            flops=8 * rows * HD * (old[5].shape[0] + new.shape[0]) if cached and spanned else 0,
            bytes_accessed=0,
            transcendentals=0,
        ),
        name="attention",
    )(facts, *operands)


def small_call(kernel, name, out_shape, facts, *operands):
    vmem = pl.BlockSpec(memory_space=pltpu.VMEM)
    return pl.pallas_call(
        kernel,
        out_shape=out_shape,
        in_specs=[pl.BlockSpec(memory_space=pltpu.SMEM)] + [vmem] * len(operands),
        out_specs=jax.tree.map(lambda _: vmem, out_shape),
        compiler_params=pltpu.CompilerParams(vmem_limit_bytes=4 * MIB),
        cost_estimate=COST,
        name=name,
    )(facts, *operands)


def cut_kernel(fact, facts_ref, keep_ref, got_ref, mine_ref, send_ref):
    half = mine_ref.shape[0]
    upper = facts_ref[fact] == 1
    low, high = (keep_ref[at, :] + got_ref[at, :] for at in (slice(0, half), slice(half, None)))
    mine_ref[...] = jnp.where(upper, high, low)
    send_ref[...] = jnp.where(upper, low, high)


def cut(fact, facts, keep, got):
    out = jax.ShapeDtypeStruct((keep.shape[0] // 2, keep.shape[1]), keep.dtype)
    return small_call(functools.partial(cut_kernel, fact), "cut", (out, out), facts, keep, got)


def join_kernel(fact, facts_ref, own_ref, got_ref, out_ref):
    half = own_ref.shape[1]
    upper = facts_ref[fact] == 1

    @pl.when(upper)
    def _():
        out_ref[:, :half] = got_ref[...]
        out_ref[:, half:] = own_ref[...]

    @pl.when(jnp.logical_not(upper))
    def _():
        out_ref[:, :half] = own_ref[...]
        out_ref[:, half:] = got_ref[...]


def join(fact, facts, own, got):
    count, half, width = own.shape
    if half % 16:
        upper = facts[fact] == 1
        return jnp.where(
            upper, jnp.concatenate([got, own], axis=1), jnp.concatenate([own, got], axis=1)
        )
    out = jax.ShapeDtypeStruct((count, 2 * half, width), own.dtype)
    return small_call(functools.partial(join_kernel, fact), "join", out, facts, own, got)


def merge_kernel(facts_ref, own_ref, got_ref, key_ref, value_ref):
    count, rows, _ = own_ref.shape
    for side in range(2):

        @pl.when(facts_ref[2] == side)
        def _():
            for k in range(count):
                for at, ref in ((2 * k + side, own_ref), (2 * k + 1 - side, got_ref)):
                    here = slice(at * rows, (at + 1) * rows)
                    key_ref[:, here] = ref[k, :, :HD].astype(jnp.float32).T.astype(key_ref.dtype)
                    value_ref[here, :] = ref[k, :, HD:]


def merge(facts, own, got):
    slots = 2 * own.shape[0] * own.shape[1]
    out = (
        jax.ShapeDtypeStruct((HD, slots), own.dtype),
        jax.ShapeDtypeStruct((slots, HD), own.dtype),
    )
    return small_call(merge_kernel, "merge", out, facts, own, got)


def pick_kernel(facts_ref, a_ref, b_ref, out_ref):
    @pl.when(facts_ref[1] == 1)
    def _():
        out_ref[...] = a_ref[...]

    @pl.when(facts_ref[1] != 1)
    def _():
        out_ref[...] = b_ref[...]


def pick(facts, a, b):
    return small_call(pick_kernel, "pick", jax.ShapeDtypeStruct(a.shape, a.dtype), facts, a, b)


def halves_kernel(blocks, tile, facts_ref, *refs):
    lhs, refs = refs[:blocks], refs[blocks:]
    w_refs, (keep_ref, send_ref) = refs[:-2], refs[-2:]
    rows, per_half = lhs[0].shape[0], blocks // 2
    upper, place = facts_ref[2] == 1, facts_ref[2] * 0
    for k in range(per_half.bit_length() - 1):
        place = place + facts_ref[3 + k] * (per_half >> (k + 1))
    both = jnp.concatenate([ref[...] for ref in lhs], axis=0)
    low = 0
    for w_ref in w_refs:

        @pl.loop(0, w_ref.shape[1] // tile)
        def _(step, low=low, w_ref=w_ref):
            at = pl.multiple_of(step * tile, tile)
            out = jnp.dot(both, w_ref[:, pl.ds(at, tile)], preferred_element_type=jnp.float32)
            here = pl.ds(pl.multiple_of(low + at, tile), tile)
            half = per_half * rows
            first = jnp.where(upper, out[half:], out[:half])
            second = jnp.where(upper, out[:half], out[half:])
            for k in range(per_half):
                to = pl.ds(pl.multiple_of((place ^ k) * rows, rows), rows)
                keep_ref[to, here] = first[k * rows : (k + 1) * rows]
                send_ref[to, here] = second[k * rows : (k + 1) * rows]

        low += w_ref.shape[1]


def halves(facts, lhs, weights):
    rows = lhs[0].shape[0] * len(lhs) // 2
    width = sum(w.shape[1] for w in weights)
    out = jax.ShapeDtypeStruct((rows, width), jnp.float32)
    vmem = pl.BlockSpec(memory_space=pltpu.VMEM)
    operands = [*lhs, *weights]
    return pl.pallas_call(
        functools.partial(halves_kernel, len(lhs), min(512, weights[0].shape[1])),
        out_shape=(out, out),
        in_specs=[pl.BlockSpec(memory_space=pltpu.SMEM)] + [vmem] * len(operands),
        out_specs=(vmem, vmem),
        compiler_params=pltpu.CompilerParams(vmem_limit_bytes=5 * MIB),
        cost_estimate=pl.CostEstimate(
            flops=4 * rows * weights[0].shape[0] * width, bytes_accessed=0, transcendentals=0
        ),
        name="halves",
    )(facts, *operands)


def pack_kernel(low, shift, where_at, facts_ref, keep_ref, got_ref, cos_ref, sin_ref, same_ref, other_ref):
    few = keep_ref.shape[0]
    cosine, sine = cos_ref[low : low + few, :], sin_ref[low : low + few, :]
    far, near = facts_ref[where_at], facts_ref[where_at + 1]
    for d in range(same_ref.shape[0]):
        for k, out_ref in enumerate((same_ref, other_ref)):
            head = ((far ^ d) * 2 + (near ^ k)) >> shift
            raw, value = (
                keep_ref[:, pl.ds(pl.multiple_of(at * HD, HD), HD)]
                + got_ref[:, pl.ds(pl.multiple_of(at * HD, HD), HD)]
                for at in (head, KV + head)
            )
            both = [raw * cosine + pltpu.roll(raw, HD // 2, 1) * sine, value]
            out_ref[d] = jnp.concatenate(both, axis=1).astype(out_ref.dtype)


def pack(low, shift, where_at, count, facts, keep, got, cosine, sine):
    out = jax.ShapeDtypeStruct((count, keep.shape[0], 2 * HD), jnp.bfloat16)
    kernel = functools.partial(pack_kernel, low, shift, where_at)
    return small_call(kernel, "pack", (out, out), facts, keep, got, cosine, sine)


def on_device(resid, norm_gain, w_query, w_key, w_value, w_out, cache_key, cache_value, prefix_len):
    blk_count, red_count = lax.axis_size("blk"), lax.axis_size("red")
    blk_at, red_at = lax.axis_index("blk"), lax.axis_index("red")
    start = prefix_len[0]
    mine, width = resid.shape
    far_count = blk_count // 2
    far_at, near_at = blk_at // 2, blk_at % 2
    bits = [1 << k for k in range(red_count.bit_length() - 1)]

    def swap_red(value, bit):
        return lax.ppermute(value, "red", [(k, k ^ bit) for k in range(red_count)])

    def swap_near(value):
        return lax.ppermute(value, "blk", [(k, k ^ 1) for k in range(blk_count)])

    def move_far(value, pairs):
        pairs = [(2 * a + k, 2 * b + k) for a, b in pairs for k in range(2)]
        return lax.ppermute(value, "blk", pairs)

    line = far_count == 4
    if line:
        at_end = (far_at == 0) | (far_at == 3)
        pairs_out = [(1, 0), (2, 3)]
        pairs_in = [(0, 1), (3, 2)]
        middle = [(1, 2), (2, 1)]
        owners = [
            far_at,
            far_at ^ 1,
            far_at ^ jnp.where(at_end, 2, 3),
            far_at ^ jnp.where(at_end, 3, 2),
        ]
    else:
        owners = [(far_at + j) % far_count for j in range(far_count)]

    def spread(own):
        if not line:
            ring = range(far_count)
            return [move_far(own, [((k + j) % far_count, k) for k in ring]) for j in ring if j > 0]
        a1 = move_far(own, pairs_out + pairs_in)
        b1 = move_far(own, middle)
        return [a1, b1, move_far(b1, pairs_out), move_far(a1, middle)]

    def arrive(hops, facts, *others):
        if not line:
            return hops
        a1, b1, a2, b2 = hops
        a3 = move_far(after(b2, *others), pairs_out)
        return [a1, pick(facts, a2, b1), pick(facts, a3, b2)]

    wide = lambda value: value.astype(jnp.float32)

    def add(terms, *others):
        return sum(map(wide, [*terms[:-1], after(terms[-1], *others)])).astype(jnp.float16)

    def collect(parts, first):
        own = [list(terms) for terms in parts[0]]
        if line:
            a1 = [move_far(value, pairs_out + pairs_in) for value in first]
            s2, s3 = parts[2:]
            last = first[-1]
            stages = {}

            def go(name, terms, pairs):
                nonlocal last
                last = add(terms, last)
                stages[name] = move_far(last, pairs)

            go("a3", s3[0], pairs_in)
            go("a3+", s3[1], pairs_in)
            go("b2", s3[0] + [stages["a3"]], middle)
            go("a2", s2[0], pairs_in)
            go("b2+", s3[1] + [stages["a3+"]], middle)
            go("c1", [stages["b2"]], pairs_out)
            go("a2+", s2[1], pairs_in)
            go("b1", s2[0] + [stages["a2"]], middle)
            go("c1+", [stages["b2+"]], pairs_out)
            go("b1+", s2[1] + [stages["a2+"]], middle)
            for k, end in enumerate(("", "+")):
                own[k] += [a1[k], stages["c1" + end], stages["b1" + end]]
        else:
            ring = range(far_count)
            for j in ring:
                for k, terms in enumerate(parts[j] if j > 0 else []):
                    own[k].append(
                        move_far(add(terms), [(i, (i + j) % far_count) for i in ring])
                    )
        return [sum(map(wide, terms)) for terms in own]

    def after(value, *others):
        return lax.optimization_barrier((value, *others))[0] if others else value

    def side_of(bit):
        return (red_at // bit) % 2

    here, few = 2 * mine // red_count, mine // red_count
    low = sum(side_of(bit) * (mine >> k) for k, bit in enumerate(bits) if k > 0)
    bases = [(owner * 2 + (near_at ^ side_of(1))) * mine + low for owner in owners]
    few_low = sum(side_of(bit) * (mine >> (k + 1)) for k, bit in enumerate(bits))
    end = at_end.astype(jnp.int32) if line else jnp.int32(0)
    base_at = 4 + len(bits)
    facts = [start, end, *map(side_of, bits), far_at, near_at, *bases, blk_at * mine + few_low]
    facts = jnp.stack(facts).astype(jnp.int32)

    def sum_rows(keep, got):
        for k, bit in enumerate(bits[1:]):
            keep, send = cut(3 + k, facts, keep, got)
            got = swap_red(send, bit)
        return keep, got

    def join_rows(value, which, *others):
        for k in reversed(which):
            got = after(swap_red(value, bits[k]), *others)
            value = join(2 + k, facts, value, got)
        return value

    head_at = blk_at // (blk_count // KV)
    one_head = lambda value: lax.dynamic_slice_in_dim(value, head_at * HD, HD, 1)
    cached = jnp.concatenate([one_head(cache_key), one_head(cache_value)], axis=1)

    token_at = (facts[base_at:-1, None] + jnp.arange(here, dtype=jnp.int32)).reshape(-1)
    few_at = facts[-1] + jnp.arange(few, dtype=jnp.int32)
    cosine, sine = tables(start + jnp.concatenate([token_at, few_at]))

    total_sq = jnp.sum(resid * resid, axis=1)
    for bit in bits:
        total_sq = total_sq + after(swap_red(total_sq, bit), facts)
    normed = (
        resid * lax.rsqrt(total_sq[:, None] / (width * red_count) + 1e-05) * norm_gain[None, :]
    ).astype(jnp.bfloat16)

    def pieces_of(value):
        return jnp.split(value, PIECES, axis=1)

    slots = range(far_count)
    last = far_count - 1
    hops = spread(normed)
    near = [swap_near(normed)]

    def ask(j, *others):
        return halves(facts, [after(far[j], *others), near[j]], [w_query])

    def have(*hops):
        return hops if line else ()

    def reduce(pair, got, *others):
        return sum_rows(after(pair[0], *others), got)

    def core(pair):
        return swap_red(pair[1], bits[0])

    half = mine // 2
    rest = range(1, len(bits))
    cached = after(cached, normed)[None]
    kv = halves(facts, [normed[:half], normed[half:]], [w_key, w_value])
    cached = join_rows(cached, rest, near[0], kv[0])
    cached = cached.reshape(red_count // 2, -1, 2 * HD)
    kv = reduce(kv, core(kv), near[0], hops[0], *have(hops[1]))
    shift = (blk_count // KV).bit_length() - 1
    same, other = pack(
        far_count * here, shift, base_at - 2, far_count, facts, *kv, cosine, sine
    )
    other = swap_near(other)
    far = [normed]
    asked = [ask(0, same, hops[0], *have(hops[1]))]
    far += arrive(hops, facts, asked[0][0])
    near += [swap_near(far[j]) for j in slots[1:]]
    moved = [core(asked[0])]
    keys, values = merge(facts, cached, after(swap_red(cached, bits[0]), asked[0][0]))
    fresh = jnp.stack([same, after(other, asked[0][0])], axis=1)
    fresh = [fresh[0]] + [
        move_far(fresh[d], [(k, k ^ d) for k in range(far_count)]) for d in range(1, far_count)
    ]
    asked.append(ask(1, keys, far[2], fresh[0], *have(hops[-1])))
    moved.append(core(asked[1]))
    fresh = lax.optimization_barrier((*fresh, asked[1][0]))[:-1]
    fresh = jnp.concatenate(fresh)
    asked[0] = reduce(asked[0], moved[0], asked[1][0])
    for j in range(2, last):
        asked.append(ask(j, asked[j - 2][0], far[j + 1], fresh))
        moved.append(core(asked[j]))
        if j < last - 1:
            asked[j - 1] = reduce(asked[j - 1], moved[j - 1], asked[j][0])
    rows = here * (w_query.shape[1] // HD)

    def mix(j, new, *others):
        keep, got = asked[j]
        old = [after(keep, *others), got, cosine, sine, keys, values]
        return attend(base_at, far_count, j, facts, here, rows, old, new)

    rest = range(1, len(bits))
    fresh = join_rows(fresh, rest, asked[last - 1][0])
    asked[last - 2] = reduce(asked[last - 2], moved[last - 2], fresh)
    begun = mix(0, None, asked[last - 2][0], fresh)
    fresh = join_rows(fresh, [0], begun[2]).reshape(blk_count * mine, 2 * HD)
    mixed = [None] * far_count
    mixed[0] = attend(base_at, far_count, 0, facts, here, rows, begun, fresh)
    asked.append(ask(last, mixed[0], asked[last - 2][1]))
    moved.append(core(asked[last]))

    parts = [None] * far_count
    per_half = red_count // 2
    turns = [
        sum(bit for i, bit in enumerate(bits[1:]) if k & (per_half >> (i + 1)))
        for k in range(per_half)
    ]
    turns = turns + [turn | bits[0] for turn in turns]

    def share(j):
        return [swap_red(mixed[j], turn) if turn else mixed[j] for turn in turns]

    def project(j, blocks, *others):
        blocks = [after(blocks[0], *others), *blocks[1:]]
        return halves(facts, blocks, [w_out])

    def finish(j, pair, *others):
        keep, send = pair
        send = after(send, *others)
        send = (send * SHRINK).astype(jnp.float16)
        send = [send] if j == 0 else pieces_of(send)
        got = [swap_near(p) for p in send]
        pieces = pieces_of(got[0]) if j == 0 else got
        parts[j] = [[p * SHRINK, g] for p, g in zip(pieces_of(keep), pieces)]
        return send, got

    shared = {0: share(0)}
    asked[last] = reduce(asked[last], moved[last])
    asked[last - 1] = reduce(asked[last - 1], moved[last - 1], asked[last][0])
    mixed[1] = mix(1, fresh, asked[last - 1][0])
    shared[1] = share(1)
    done, got = finish(0, project(0, shared[0], mixed[1], asked[last][1]))
    mixed[last] = mix(last, fresh, *done)
    shared[last] = share(last)
    done, got1 = finish(1, project(1, shared[1], mixed[last]))
    done = [*done, *got]
    for j in range(2, last):
        mixed[j] = mix(j, fresh, *done)
        shared[j] = share(j)
        done = [mixed[j]]
    first = [add(parts[1][0], *done)]
    first.append(add(parts[1][1], first[0]))
    done, _ = finish(last, project(last, shared[last], *done, *first))
    for j in range(2, last):
        done, _ = finish(j, project(j, shared[j], *done))
    return resid + jnp.concatenate(collect(parts, first), axis=1) * (1.0 / SHRINK)


def solution(mesh):
    placed = (
        P("blk", "red"),
        P("red"),
        P("red", "blk"),
        P("red", None),
        P("red", None),
        P("blk", "red"),
        P("red", None),
        P("red", None),
        P(),
    )
    return jax.shard_map(
        on_device, mesh=mesh, in_specs=placed, out_specs=P("blk", "red"), check_vma=False
    )
```

time: 781 us -> 348 us (0.45)
  waiting for transfers between devices: 518 us -> 124 us
  matrix products: 157 us -> 0 us
  Pallas kernels: 0 us -> 125 us
  starting transfers between devices: 0.21 us -> 59.3 us
  other arithmetic: 60.1 us -> 8.49 us
  blocking collectives: 20.3 us -> 0 us
  between operations: 14.3 us -> 1.89 us
  local copies, waits for them, and re-layouts: 10.3 us -> 22.2 us
    reduce_scatter x2 -> x0, waiting for transfers between devices: 354 us -> none  [the longest x1 283 us: on_device(): summed = lax.psum_scatter(out_terms, 'blk', scatter_dimension=0, tiled=True)]
    all_gather x4 -> x0, waiting for transfers between devices: 164 us -> none  [the longest x1 124 us: on_device(): lax.all_gather(normed, 'blk', axis=0, tiled=True)]
    dot_general x6 -> x0, matrix products: 157 us -> none  [the longest x1 46.1 us: on_device(): jnp.einsum('tgd,cd->tgc', query, all_ck, preferred_element_type=jnp.float32)]
    pallas_call x0 -> x26, Pallas kernels: none -> 125 us  [the longest x5 59.9 us: attend(): pl.pallas_call(functools.partial(attention_kernel, base_at, far_count, sl...]
    ppermute x0 -> x60, waiting for transfers between devices: none -> 124 us  [the longest x12 50.9 us: swap_near(): return lax.ppermute(value, 'blk', [(k, k ^ 1) for k in range(blk_count)])]
    ppermute x0 -> x60, starting transfers between devices: none -> 59.3 us  [the longest x20 26.7 us: move_far(): return lax.ppermute(value, 'blk', pairs)]
    reduce_sum x3 -> x1, other arithmetic: 51.3 us -> 1.82 us  [on_device(): total_sq = jnp.sum(resid * resid, axis=1)]
    unnamed x5 -> x35, local copies, waits for them, and re-layouts: 3.12 us -> 19.9 us
  transfers between devices with their start and end apart: 6 -> 60, of which waited for: 5 -> 22; matrix products, arithmetic and copies ran while one was open for 15% -> 2% of each run, Pallas kernels for 0% -> 35%
where the time goes in v2:
time: 348 us; the launch traced here: 342 us
  Pallas kernels  125 us (36%)
  waiting for transfers between devices  124 us (36%)
  starting transfers between devices  59.3 us (17%)
  local copies, waits for them, and re-layouts  22.2 us (6%)
  other arithmetic  8.49 us (2%)
    pallas_call x5, Pallas kernels, attend(): pl.pallas_call(functools.partial(attention_kernel, base_at, far_count, sl...  59.9 us
    pallas_call x9, Pallas kernels, halves(): pl.pallas_call(functools.partial(halves_kernel, len(lhs), min(512, weight...  54.3 us
    ppermute x12, waiting for transfers between devices, swap_near(): return lax.ppermute(value, 'blk', [(k, k ^ 1) for k in range(blk_count)])  50.9 us
    ppermute x20, waiting for transfers between devices, move_far(): return lax.ppermute(value, 'blk', pairs)  48.7 us
    ppermute x20, starting transfers between devices, move_far(): return lax.ppermute(value, 'blk', pairs)  26.7 us
    ppermute x28, waiting for transfers between devices, swap_red(): return lax.ppermute(value, 'red', [(k, k ^ bit) for k in range(red_count)])  24.8 us
    ppermute x28, starting transfers between devices, swap_red(): return lax.ppermute(value, 'red', [(k, k ^ bit) for k in range(red_count)])  20.3 us
    unnamed x35, local copies, waits for them, and re-layouts  19.9 us
  transfers between devices with their start and end apart: 60, of which 22 were waited for; matrix products, arithmetic and copies ran while one was open for 2% of the time, Pallas kernels for 35%

profile of v2, /device:TPU:0, one launch (start us, length us, event | category | flops | bytes accessed | tf_op | source)
XLA Modules:
  0.0 341.6 jit_solution(8207691011946317480)
XLA Ops:
  0.0 1.8 multiply_reduce_fusion
  3.0 1.4 constant_dynamic-slice_fusion
  4.6 2.7 collective-permute-start.1
  7.3 1.4 collective-permute-done.1
  9.1 2.1 collective-permute-start.2
  11.1 1.6 collective-permute-start.3
  12.7 1.5 collective-permute-start.7
  14.3 1.7 collective-permute-start.4
  16.0 3.4 copy-done.3
  19.4 3.4 copy-done.4
  22.8 4.3 %halves.9 = (f32[64,2048]{1,0:T(8,128)S(1)}, f32[64,2048]{1,0:T(8,128)}) custom-call(s32[11]{0:T(128)S(1)} %stack.58.facts_ref.refs_0_, bf16[64,4096]{1,0:T(8,128)(2,1)S(1)} %get-tuple-element.166.refs_0_, bf16[64,4096]{1,0:T(8,128)(2,1)S(1)} %get-tuple-element.165.refs_1_, bf16[4096,1024]{1,0:T(8,128)(2,1)S(1)} %copy-done.3, bf16[4096,1024]{1,0:T(8,128)(2,1)S(1)} %copy-done.4), custom_call_target="tpu_custom_call" | custom-call | flops 2147483648 | tf_op jit(solution)/shard_map/halves/pallas_call | solution.py:293
  27.1 6.6 %collective-permute-done.2.refs_1_ = bf16[128,4096]{1,0:T(8,128)(2,1)S(1)} collective-permute-done((bf16[128,4096]{1,0:T(8,128)(2,1)S(1)}, bf16[128,4096]{1,0:T(8,128)(2,1)S(1)}, u32[]{:S(2)}, u32[]{:S(2)}) %collective-permute-start.2) | collective-permute-done | bytes 1048608 | tf_op jit(solution)/shard_map/ppermute | solution.py:341
  33.7 2.7 collective-permute-done.7.got_ref
  38.9 3.2 collective-permute-done.5.got_ref
  44.3 1.6 collective-permute-start.6
  48.5 4.4 %collective-permute-done.6.got_ref = f32[32,2048]{1,0:T(8,128)S(1)} collective-permute-done((f32[32,2048]{1,0:T(8,128)S(1)}, f32[32,2048]{1,0:T(8,128)S(1)}, u32[]{:S(2)}, u32[]{:S(2)}) %collective-permute-start.6) | collective-permute-done | bytes 262176 | tf_op jit(solution)/shard_map/ppermute | solution.py:338
  53.6 5.8 %copy-done = bf16[4096,2048]{1,0:T(8,128)(2,1)S(1)} copy-done((bf16[4096,2048]{1,0:T(8,128)(2,1)S(1)}, bf16[4096,2048]{1,0:T(8,128)(2,1)}, u32[]{:S(2)}) %copy-start) | copy-done | bytes 16777240
  59.4 5.8 %halves.10 = (f32[128,2048]{1,0:T(8,128)S(1)}, f32[128,2048]{1,0:T(8,128)S(1)}) custom-call(s32[11]{0:T(128)S(1)} %stack.58.facts_ref.refs_0_, bf16[128,4096]{1,0:T(8,128)(2,1)S(1)} %multiply_convert_fusion.4.refs_0_, bf16[128,4096]{1,0:T(8,128)(2,1)S(1)} %copy-done.6, bf16[4096,2048]{1,0:T(8,128)(2,1)S(1)} %copy-done), custom_call_target="tpu_custom_call" | custom-call | flops 4294967296 | tf_op jit(solution)/shard_map/halves/pallas_call | solution.py:293
  65.2 1.3 collective-permute-start.18
  67.1 6.9 %collective-permute-done.10 = bf16[4,32,256]{2,1,0:T(8,128)(2,1)S(1)} collective-permute-done((bf16[4,32,256]{2,1,0:T(8,128)(2,1)S(1)}, bf16[4,32,256]{2,1,0:T(8,128)(2,1)S(1)}, u32[]{:S(2)}, u32[]{:S(2)}) %collective-permute-start.10) | collective-permute-done | bytes 65568 | tf_op jit(solution)/shard_map/ppermute | solution.py:341
  74.1 1.3 pick.2.refs_0_
  76.0 2.5 merge.1
  78.5 5.8 %copy-done.1 = bf16[4096,2048]{1,0:T(8,128)(2,1)S(1)} copy-done((bf16[4096,2048]{1,0:T(8,128)(2,1)S(1)}, bf16[4096,2048]{1,0:T(8,128)(2,1)}, u32[]{:S(2)}) %copy-start.1) | copy-done | bytes 16777240
  84.3 6.6 %halves.11 = (f32[128,2048]{1,0:T(8,128)S(1)}, f32[128,2048]{1,0:T(8,128)S(1)}) custom-call(s32[11]{0:T(128)S(1)} %stack.58.facts_ref.refs_0_, bf16[128,4096]{1,0:T(8,128)(2,1)} %collective-permute-done.3.refs_0_, bf16[128,4096]{1,0:T(8,128)(2,1)S(1)} %collective-permute-done.12.refs_1_, bf16[4096,2048]{1,0:T(8,128)(2,1)S(1)} %copy-done.1), custom_call_target="tpu_custom_call" | custom-call | flops 4294967296 | tf_op jit(solution)/shard_map/halves/pallas_call | solution.py:293
  91.2 2.4 collective-permute-start.14
  93.6 2.7 collective-permute-done.14
  96.3 2.2 collective-permute-start.15
  98.6 2.6 collective-permute-done.15
  101.1 2.5 collective-permute-start.16
  103.6 3.2 collective-permute-done.16
  109.8 1.6 collective-permute-start.21
  111.4 5.8 %halves.12 = (f32[128,2048]{1,0:T(8,128)S(1)}, f32[128,2048]{1,0:T(8,128)S(1)}) custom-call(s32[11]{0:T(128)S(1)} %stack.58.facts_ref.refs_0_, bf16[128,4096]{1,0:T(8,128)(2,1)S(1)} %pick.2.refs_0_, bf16[128,4096]{1,0:T(8,128)(2,1)S(1)} %collective-permute-done.19.refs_1_, bf16[4096,2048]{1,0:T(8,128)(2,1)S(1)} %copy-done.2), custom_call_target="tpu_custom_call" | custom-call | flops 4294967296 | tf_op jit(solution)/shard_map/halves/pallas_call | solution.py:293
  119.0 7.3 %collective-permute-done.21.refs_2_ = f32[64,2048]{1,0:T(8,128)S(1)} collective-permute-done((f32[64,2048]{1,0:T(8,128)S(1)}, f32[64,2048]{1,0:T(8,128)S(1)}, u32[]{:S(2)}, u32[]{:S(2)}) %collective-permute-start.21) | collective-permute-done | bytes 524320 | tf_op jit(solution)/shard_map/ppermute | solution.py:338
  126.3 13.4 %attention.5 = (bf16[1024,128]{1,0:T(8,128)(2,1)S(1)}, f32[1024,128]{1,0:T(8,128)S(1)}, f32[1024,256]{1,0:T(8,128)S(1)}) custom-call(s32[11]{0:T(128)S(1)} %stack.58.facts_ref.refs_0_, f32[64,2048]{1,0:T(8,128)S(1)} %get-tuple-element.113.refs_1_, f32[64,2048]{1,0:T(8,128)S(1)} %collective-permute-done.21.refs_2_, ...), custom_call_target="tpu_custom_call" | custom-call | tf_op jit(solution)/shard_map/attention/pallas_call | solution.py:156
  140.6 2.4 attention.6.refs_0_
  143.1 5.8 %halves.13 = (f32[128,2048]{1,0:T(8,128)S(1)}, f32[128,2048]{1,0:T(8,128)S(1)}) custom-call(s32[11]{0:T(128)S(1)} %stack.58.facts_ref.refs_0_, bf16[128,4096]{1,0:T(8,128)(2,1)S(1)} %pick.3.refs_0_, bf16[128,4096]{1,0:T(8,128)(2,1)S(1)} %collective-permute-done.24.refs_1_, bf16[4096,2048]{1,0:T(8,128)(2,1)S(1)} %copy-done.2), custom_call_target="tpu_custom_call" | custom-call | flops 4294967296 | tf_op jit(solution)/shard_map/halves/pallas_call | solution.py:293
  150.0 1.6 collective-permute-start.30
  154.4 14.7 %attention.7.refs_0_ = bf16[64,2048]{1,0:T(8,128)(2,1)S(1)} custom-call(s32[11]{0:T(128)S(1)} %stack.58.facts_ref.refs_0_, f32[64,2048]{1,0:T(8,128)S(1)} %get-tuple-element.128.refs_1_, f32[64,2048]{1,0:T(8,128)S(1)} %collective-permute-done.23.refs_2_, f32[288,128]{1,0:T(8,128)S(1)} %get-tuple-element.176.cos_ref.refs_3_, ...), custom_call_target="tpu_custom_call" | custom-call | flops 9663676416 | tf_op jit(solution)/shard_map/attention/pallas_call | solution.py:156
  169.1 1.6 collective-permute-start.32
  170.7 4.8 %collective-permute-done.27.refs_2_ = f32[64,2048]{1,0:T(8,128)S(1)} collective-permute-done((f32[64,2048]{1,0:T(8,128)S(1)}, f32[64,2048]{1,0:T(8,128)S(1)}, u32[]{:S(2)}, u32[]{:S(2)}) %collective-permute-start.27) | collective-permute-done | bytes 524320 | tf_op jit(solution)/shard_map/ppermute | solution.py:338
  176.1 1.5 collective-permute-start.36
  177.7 6.5 %halves.14 = (f32[128,4096]{1,0:T(8,128)S(1)}, f32[128,4096]{1,0:T(8,128)S(1)}) custom-call(s32[11]{0:T(128)S(1)} %stack.58.facts_ref.refs_0_, bf16[64,2048]{1,0:T(8,128)(2,1)S(1)} %attention.6.refs_0_, bf16[64,2048]{1,0:T(8,128)(2,1)S(1)} %collective-permute-done.28.refs_1_, bf16[64,2048]{1,0:T(8,128)(2,1)S(1)} %collective-permute-done.29.refs_2_, ...), custom_call_target="tpu_custom_call" | custom-call | flops 4294967296 | tf_op jit(solution)/shard_map/halves/pallas_call | solution.py:293
  185.5 14.7 %attention.8.refs_0_ = bf16[64,2048]{1,0:T(8,128)(2,1)S(1)} custom-call(s32[11]{0:T(128)S(1)} %stack.58.facts_ref.refs_0_, f32[64,2048]{1,0:T(8,128)S(1)} %get-tuple-element.133.refs_1_, f32[64,2048]{1,0:T(8,128)S(1)} %collective-permute-done.27.refs_2_, f32[288,128]{1,0:T(8,128)S(1)} %get-tuple-element.176.cos_ref.refs_3_, ...), custom_call_target="tpu_custom_call" | custom-call | flops 9663676416 | tf_op jit(solution)/shard_map/attention/pallas_call | solution.py:156
  200.8 6.5 %halves.15 = (f32[128,4096]{1,0:T(8,128)S(1)}, f32[128,4096]{1,0:T(8,128)S(1)}) custom-call(s32[11]{0:T(128)S(1)} %stack.58.facts_ref.refs_0_, bf16[64,2048]{1,0:T(8,128)(2,1)S(1)} %attention.7.refs_0_, bf16[64,2048]{1,0:T(8,128)(2,1)S(1)} %collective-permute-done.32.refs_1_, bf16[64,2048]{1,0:T(8,128)(2,1)S(1)} %collective-permute-done.33.refs_2_, ...), custom_call_target="tpu_custom_call" | custom-call | flops 4294967296 | tf_op jit(solution)/shard_map/halves/pallas_call | solution.py:293
  210.9 14.7 %attention.9.refs_0_ = bf16[64,2048]{1,0:T(8,128)(2,1)S(1)} custom-call(s32[11]{0:T(128)S(1)} %stack.58.facts_ref.refs_0_, f32[64,2048]{1,0:T(8,128)S(1)} %get-tuple-element.137.refs_1_, f32[64,2048]{1,0:T(8,128)S(1)} %collective-permute-done.36.refs_2_, f32[288,128]{1,0:T(8,128)S(1)} %get-tuple-element.176.cos_ref.refs_3_, ...), custom_call_target="tpu_custom_call" | custom-call | flops 9663676416 | tf_op jit(solution)/shard_map/attention/pallas_call | solution.py:156
  226.4 7.0 %collective-permute-done.38 = f16[128,2048]{1,0:T(8,128)(2,1)S(1)} collective-permute-done((f16[128,2048]{1,0:T(8,128)(2,1)S(1)}, f16[128,2048]{1,0:T(8,128)(2,1)S(1)}, u32[]{:S(2)}, u32[]{:S(2)}) %collective-permute-start.38) | collective-permute-done | bytes 524320 | tf_op jit(solution)/shard_map/ppermute | solution.py:341
  233.6 1.7 collective-permute-start.49
  235.3 6.5 %halves.16 = (f32[128,4096]{1,0:T(8,128)S(1)}, f32[128,4096]{1,0:T(8,128)S(1)}) custom-call(s32[11]{0:T(128)S(1)} %stack.58.facts_ref.refs_0_, bf16[64,2048]{1,0:T(8,128)(2,1)S(1)} %attention.8.refs_0_, bf16[64,2048]{1,0:T(8,128)(2,1)S(1)} %collective-permute-done.39.refs_1_, bf16[64,2048]{1,0:T(8,128)(2,1)S(1)} %collective-permute-done.40.refs_2_, ...), custom_call_target="tpu_custom_call" | custom-call | flops 4294967296 | tf_op jit(solution)/shard_map/halves/pallas_call | solution.py:293
  244.3 6.5 %halves.17 = (f32[128,4096]{1,0:T(8,128)S(1)}, f32[128,4096]{1,0:T(8,128)S(1)}) custom-call(s32[11]{0:T(128)S(1)} %stack.58.facts_ref.refs_0_, bf16[64,2048]{1,0:T(8,128)(2,1)S(1)} %attention.9.refs_0_, bf16[64,2048]{1,0:T(8,128)(2,1)S(1)} %collective-permute-done.47.refs_1_, bf16[64,2048]{1,0:T(8,128)(2,1)S(1)} %collective-permute-done.48.refs_2_, ...), custom_call_target="tpu_custom_call" | custom-call | flops 4294967296 | tf_op jit(solution)/shard_map/halves/pallas_call | solution.py:293
  251.0 6.0 %collective-permute-done.42 = f16[128,2048]{1,0:T(8,128)(2,1)S(1)} collective-permute-done((f16[128,2048]{1,0:T(8,128)(2,1)S(1)}, f16[128,2048]{1,0:T(8,128)(2,1)S(1)}, u32[]{:S(2)}, u32[]{:S(2)}) %collective-permute-start.42) | collective-permute-done | bytes 524320 | tf_op jit(solution)/shard_map/ppermute | solution.py:341
  257.2 1.4 collective-permute-start.43
  258.8 1.6 collective-permute-start.50
  260.8 7.4 %collective-permute-done.44 = f16[128,2048]{1,0:T(8,128)(2,1)S(1)} collective-permute-done((f16[128,2048]{1,0:T(8,128)(2,1)S(1)}, f16[128,2048]{1,0:T(8,128)(2,1)S(1)}, u32[]{:S(2)}, u32[]{:S(2)}) %collective-permute-start.44) | collective-permute-done | bytes 524320 | tf_op jit(solution)/shard_map/ppermute | solution.py:341
  268.4 1.4 collective-permute-start.46
  270.8 8.7 %collective-permute-done.50 = f16[128,2048]{1,0:T(8,128)(2,1)S(1)} collective-permute-done((f16[128,2048]{1,0:T(8,128)(2,1)S(1)}, f16[128,2048]{1,0:T(8,128)(2,1)S(1)}, u32[]{:S(2)}, u32[]{:S(2)}) %collective-permute-start.50) | collective-permute-done | bytes 524320 | tf_op jit(solution)/shard_map/ppermute | solution.py:341
  279.7 1.4 collective-permute-start.52
  282.0 7.7 %collective-permute-done.53 = f16[128,2048]{1,0:T(8,128)(2,1)S(1)} collective-permute-done((f16[128,2048]{1,0:T(8,128)(2,1)S(1)}, f16[128,2048]{1,0:T(8,128)(2,1)S(1)}, u32[]{:S(2)}, u32[]{:S(2)}) %collective-permute-start.53) | collective-permute-done | bytes 524320 | tf_op jit(solution)/shard_map/ppermute | solution.py:341
  289.9 1.4 collective-permute-start.58
  291.4 2.0 collective-permute-start.37
  295.7 8.0 %collective-permute-done.58 = f16[128,2048]{1,0:T(8,128)(2,1)S(1)} collective-permute-done((f16[128,2048]{1,0:T(8,128)(2,1)S(1)}, f16[128,2048]{1,0:T(8,128)(2,1)S(1)}, u32[]{:S(2)}, u32[]{:S(2)}) %collective-permute-start.58) | collective-permute-done | bytes 524320 | tf_op jit(solution)/shard_map/ppermute | solution.py:345
  305.2 9.7 %collective-permute-done.55 = f16[128,2048]{1,0:T(8,128)(2,1)S(1)} collective-permute-done((f16[128,2048]{1,0:T(8,128)(2,1)S(1)}, f16[128,2048]{1,0:T(8,128)(2,1)S(1)}, u32[]{:S(2)}, u32[]{:S(2)}) %collective-permute-start.55) | collective-permute-done | bytes 524320 | tf_op jit(solution)/shard_map/ppermute | solution.py:345
  315.6 8.9 %collective-permute-done.37 = f16[128,2048]{1,0:T(8,128)(2,1)S(1)} collective-permute-done((f16[128,2048]{1,0:T(8,128)(2,1)S(1)}, f16[128,2048]{1,0:T(8,128)(2,1)S(1)}, u32[]{:S(2)}, u32[]{:S(2)}) %collective-permute-start.37) | collective-permute-done | bytes 524320 | tf_op jit(solution)/shard_map/ppermute | solution.py:345
  324.5 13.5 %collective-permute-done.57 = f16[128,2048]{1,0:T(8,128)(2,1)S(1)} collective-permute-done((f16[128,2048]{1,0:T(8,128)(2,1)S(1)}, f16[128,2048]{1,0:T(8,128)(2,1)S(1)}, u32[]{:S(2)}, u32[]{:S(2)}) %collective-permute-start.57) | collective-permute-done | bytes 524320 | tf_op jit(solution)/shard_map/ppermute | solution.py:345
  339.6 1.5 fusion
  (155 shorter events, 39.1 us)
Async XLA Ops:
  1.8 2.7 collective-permute-start
  4.6 4.2 %collective-permute-start.1 = (f32[128]{0:T(128)S(1)}, f32[128]{0:T(128)S(1)}, u32[]{:S(2)}, u32[]{:S(2)}) collective-permute-start(f32[128]{0:T(128)S(1)} %add.187), channel_id=1, source_target_pairs={{0,2},{1,3},{2,0},{3,1},{4,6},{5,7},{6,4},{7,5},{8,10},{9,11},{10,... | collective-permute-start | bytes 1544 | tf_op jit(solution)/shard_map/ppermute | solution.py:338
  9.1 24.7 %collective-permute-start.2 = (bf16[128,4096]{1,0:T(8,128)(2,1)S(1)}, bf16[128,4096]{1,0:T(8,128)(2,1)S(1)}, u32[]{:S(2)}, u32[]{:S(2)}) collective-permute-start(bf16[128,4096]{1,0:T(8,128)(2,1)S(1)} %multiply_convert_fusion.4.refs_0_), channel_id=1, source_target_pairs={{0,4},{4,0},{8,12},{12,8},{16,20},{20,16},{24,28},{28,24},{1,5},{5... | collective-permute-start | bytes 3145736 | tf_op jit(solution)/shard_map/ppermute | solution.py:341
  11.1 26.9 %collective-permute-start.3 = (bf16[128,4096]{1,0:T(8,128)(2,1)S(1)}, bf16[128,4096]{1,0:T(8,128)(2,1)}, u32[]{:S(2)}, u32[]{:S(2)}) collective-permute-start(bf16[128,4096]{1,0:T(8,128)(2,1)S(1)} %multiply_convert_fusion.4.refs_0_), channel_id=1, source_target_pairs={{8,0},{12,4},{16,24},{20,28},{0,8},{4,12},{24,16},{28,20},{9,1},{1... | collective-permute-start | bytes 3145736 | tf_op jit(solution)/shard_map/ppermute | solution.py:345
  12.7 23.8 %collective-permute-start.7 = (bf16[1,2048,256]{2,1,0:T(8,128)(2,1)S(1)}, bf16[1,2048,256]{2,1,0:T(8,128)(2,1)S(1)}, u32[]{:S(2)}, u32[]{:S(2)}) collective-permute-start(bf16[1,2048,256]{2,1,0:T(8,128)(2,1)S(1)} %bitcast.29), channel_id=1, source_target_pairs={{0,2},{1,3},{2,0},{3,1},{4,6},{5,7},{6,4},{7,5},{8,10},{9,11},{10,... | collective-permute-start | bytes 3145736 | tf_op jit(solution)/shard_map/ppermute | solution.py:338
  14.3 24.6 %collective-permute-start.4 = (bf16[128,4096]{1,0:T(8,128)(2,1)S(1)}, bf16[128,4096]{1,0:T(8,128)(2,1)}, u32[]{:S(2)}, u32[]{:S(2)}) collective-permute-start(bf16[128,4096]{1,0:T(8,128)(2,1)S(1)} %multiply_convert_fusion.4.refs_0_), channel_id=1, source_target_pairs={{8,16},{12,20},{16,8},{20,12},{9,17},{13,21},{17,9},{21,13},{10,18... | collective-permute-start | bytes 3145736 | tf_op jit(solution)/shard_map/ppermute | solution.py:345
  37.2 38.8 %collective-permute-start.8 = (bf16[2,2048,256]{2,1,0:T(8,128)(2,1)S(1)}, bf16[2,2048,256]{2,1,0:T(8,128)(2,1)}, u32[]{:S(2)}, u32[]{:S(2)}) collective-permute-start(bf16[2,2048,256]{2,1,0:T(8,128)(2,1)S(1)} %bitcast.27), channel_id=1, source_target_pairs={{0,1},{1,0},{2,3},{3,2},{4,5},{5,4},{6,7},{7,6},{8,9},{9,8},{10,11... | collective-permute-start | bytes 6291464 | tf_op jit(solution)/shard_map/ppermute | solution.py:338
  37.3 4.8 %collective-permute-start.5 = (f32[64,2048]{1,0:T(8,128)}, f32[64,2048]{1,0:T(8,128)}, u32[]{:S(2)}, u32[]{:S(2)}) collective-permute-start(f32[64,2048]{1,0:T(8,128)} %get-tuple-element.85), channel_id=1, source_target_pairs={{0,1},{1,0},{2,3},{3,2},{4,5},{5,4},{6,7},{7,6},{8,9},{9,8},{10,11... | collective-permute-start | bytes 1572872 | tf_op jit(solution)/shard_map/ppermute | solution.py:338
  38.0 27.2 %collective-permute-start.11 = (bf16[128,4096]{1,0:T(8,128)(2,1)}, bf16[128,4096]{1,0:T(8,128)(2,1)S(1)}, u32[]{:S(2)}, u32[]{:S(2)}) collective-permute-start(bf16[128,4096]{1,0:T(8,128)(2,1)} %collective-permute-done.3.refs_0_), channel_id=1, source_target_pairs={{8,16},{12,20},{16,8},{20,12},{9,17},{13,21},{17,9},{21,13},{10,18... | collective-permute-start | bytes 3145736 | tf_op jit(solution)/shard_map/ppermute | solution.py:345
  44.3 8.7 %collective-permute-start.6 = (f32[32,2048]{1,0:T(8,128)S(1)}, f32[32,2048]{1,0:T(8,128)S(1)}, u32[]{:S(2)}, u32[]{:S(2)}) collective-permute-start(f32[32,2048]{1,0:T(8,128)S(1)} %get-tuple-element.87), channel_id=1, source_target_pairs={{0,2},{1,3},{2,0},{3,1},{4,6},{5,7},{6,4},{7,5},{8,10},{9,11},{10,... | collective-permute-start | bytes 786440 | tf_op jit(solution)/shard_map/ppermute | solution.py:338
  45.9 28.1 %collective-permute-start.9 = (bf16[128,4096]{1,0:T(8,128)(2,1)}, bf16[128,4096]{1,0:T(8,128)(2,1)S(1)}, u32[]{:S(2)}, u32[]{:S(2)}) collective-permute-start(bf16[128,4096]{1,0:T(8,128)(2,1)} %collective-permute-done.4.b_ref), channel_id=1, source_target_pairs={{8,0},{12,4},{16,24},{20,28},{9,1},{13,5},{17,25},{21,29},{10,2},{... | collective-permute-start | bytes 3145736 | tf_op jit(solution)/shard_map/ppermute | solution.py:345
  47.2 31.3 %collective-permute-start.12 = (bf16[128,4096]{1,0:T(8,128)(2,1)}, bf16[128,4096]{1,0:T(8,128)(2,1)S(1)}, u32[]{:S(2)}, u32[]{:S(2)}) collective-permute-start(bf16[128,4096]{1,0:T(8,128)(2,1)} %collective-permute-done.3.refs_0_), channel_id=1, source_target_pairs={{0,4},{4,0},{8,12},{12,8},{16,20},{20,16},{24,28},{28,24},{1,5},{5... | collective-permute-start | bytes 3145736 | tf_op jit(solution)/shard_map/ppermute | solution.py:341
  65.2 41.7 %collective-permute-start.18 = (bf16[128,4096]{1,0:T(8,128)(2,1)S(1)}, bf16[128,4096]{1,0:T(8,128)(2,1)S(1)}, u32[]{:S(2)}, u32[]{:S(2)}) collective-permute-start(bf16[128,4096]{1,0:T(8,128)(2,1)S(1)} %collective-permute-done.11.b_ref), channel_id=1, source_target_pairs={{8,0},{12,4},{16,24},{20,28},{9,1},{13,5},{17,25},{21,29},{10,2},{... | collective-permute-start | bytes 3145736 | tf_op jit(solution)/shard_map/ppermute | solution.py:345
  66.5 7.5 %collective-permute-start.10 = (bf16[4,32,256]{2,1,0:T(8,128)(2,1)S(1)}, bf16[4,32,256]{2,1,0:T(8,128)(2,1)S(1)}, u32[]{:S(2)}, u32[]{:S(2)}) collective-permute-start(bf16[4,32,256]{2,1,0:T(8,128)(2,1)S(1)} %get-tuple-element.95), channel_id=1, source_target_pairs={{0,4},{4,0},{8,12},{12,8},{16,20},{20,16},{24,28},{28,24},{1,5},{5... | collective-permute-start | bytes 196616 | tf_op jit(solution)/shard_map/ppermute | solution.py:341
  74.0 35.1 %collective-permute-start.13 = (f32[128,2048]{1,0:T(8,128)S(1)}, f32[128,2048]{1,0:T(8,128)S(1)}, u32[]{:S(2)}, u32[]{:S(2)}) collective-permute-start(f32[128,2048]{1,0:T(8,128)S(1)} %get-tuple-element.100), channel_id=1, source_target_pairs={{0,1},{1,0},{2,3},{3,2},{4,5},{5,4},{6,7},{7,6},{8,9},{9,8},{10,11... | collective-permute-start | bytes 3145736 | tf_op jit(solution)/shard_map/ppermute | solution.py:338
  75.4 36.0 %collective-permute-start.19 = (bf16[128,4096]{1,0:T(8,128)(2,1)S(1)}, bf16[128,4096]{1,0:T(8,128)(2,1)S(1)}, u32[]{:S(2)}, u32[]{:S(2)}) collective-permute-start(bf16[128,4096]{1,0:T(8,128)(2,1)S(1)} %pick.2.refs_0_), channel_id=1, source_target_pairs={{0,4},{4,0},{8,12},{12,8},{16,20},{20,16},{24,28},{28,24},{1,5},{5... | collective-permute-start | bytes 3145736 | tf_op jit(solution)/shard_map/ppermute | solution.py:341
  84.3 27.1 %copy-start.2 = (bf16[4096,2048]{1,0:T(8,128)(2,1)S(1)}, bf16[4096,2048]{1,0:T(8,128)(2,1)}, u32[]{:S(2)}) copy-start(bf16[4096,2048]{1,0:T(8,128)(2,1)} %refs_2_.9) | copy-start | bytes 50331652
  90.9 26.8 %collective-permute-start.20 = (f32[128,2048]{1,0:T(8,128)S(1)}, f32[128,2048]{1,0:T(8,128)S(1)}, u32[]{:S(2)}, u32[]{:S(2)}) collective-permute-start(f32[128,2048]{1,0:T(8,128)S(1)} %get-tuple-element.111), channel_id=1, source_target_pairs={{0,1},{1,0},{2,3},{3,2},{4,5},{5,4},{6,7},{7,6},{8,9},{9,8},{10,11... | collective-permute-start | bytes 3145736 | tf_op jit(solution)/shard_map/ppermute | solution.py:338
  91.2 5.1 %collective-permute-start.14 = (bf16[2,32,256]{2,1,0:T(8,128)(2,1)S(1)}, bf16[2,32,256]{2,1,0:T(8,128)(2,1)S(1)}, u32[]{:S(2)}, u32[]{:S(2)}) collective-permute-start(bf16[2,32,256]{2,1,0:T(8,128)(2,1)S(1)} %get-tuple-element.169), channel_id=1, source_target_pairs={{0,8},{4,12},{8,0},{12,4},{16,24},{20,28},{24,16},{28,20},{1,9},{5... | collective-permute-start | bytes 98312 | tf_op jit(solution)/shard_map/ppermute | solution.py:345
  96.3 4.8 %collective-permute-start.15 = (bf16[2,32,256]{2,1,0:T(8,128)(2,1)S(1)}, bf16[2,32,256]{2,1,0:T(8,128)(2,1)S(1)}, u32[]{:S(2)}, u32[]{:S(2)}) collective-permute-start(bf16[2,32,256]{2,1,0:T(8,128)(2,1)S(1)} %get-tuple-element.170), channel_id=1, source_target_pairs={{0,16},{4,20},{8,24},{12,28},{16,0},{20,4},{24,8},{28,12},{1,17},{... | collective-permute-start | bytes 98312 | tf_op jit(solution)/shard_map/ppermute | solution.py:345
  101.1 5.7 %collective-permute-start.16 = (bf16[2,32,256]{2,1,0:T(8,128)(2,1)S(1)}, bf16[2,32,256]{2,1,0:T(8,128)(2,1)S(1)}, u32[]{:S(2)}, u32[]{:S(2)}) collective-permute-start(bf16[2,32,256]{2,1,0:T(8,128)(2,1)S(1)} %get-tuple-element.167), channel_id=1, source_target_pairs={{0,24},{4,28},{8,16},{12,20},{16,8},{20,12},{24,0},{28,4},{1,25},{... | collective-permute-start | bytes 98312 | tf_op jit(solution)/shard_map/ppermute | solution.py:345
  107.5 35.6 %collective-permute-start.24 = (bf16[128,4096]{1,0:T(8,128)(2,1)S(1)}, bf16[128,4096]{1,0:T(8,128)(2,1)S(1)}, u32[]{:S(2)}, u32[]{:S(2)}) collective-permute-start(bf16[128,4096]{1,0:T(8,128)(2,1)S(1)} %pick.3.refs_0_), channel_id=1, source_target_pairs={{0,4},{4,0},{8,12},{12,8},{16,20},{20,16},{24,28},{28,24},{1,5},{5... | collective-permute-start | bytes 3145736 | tf_op jit(solution)/shard_map/ppermute | solution.py:341
  108.5 8.6 %collective-permute-start.17 = (bf16[8,32,256]{2,1,0:T(8,128)(2,1)S(1)}, bf16[8,32,256]{2,1,0:T(8,128)(2,1)S(1)}, u32[]{:S(2)}, u32[]{:S(2)}) collective-permute-start(bf16[8,32,256]{2,1,0:T(8,128)(2,1)S(1)} %constant_dynamic-update-slice_fusion.own_ref), channel_id=1, source_target_pairs={{0,2},{1,3},{2,0},{3,1},{4,6},{5,7},{6,4},{7,5},{8,10},{9,11},{10,... | collective-permute-start | bytes 393224 | tf_op jit(solution)/shard_map/ppermute | solution.py:338
  109.8 16.5 %collective-permute-start.21 = (f32[64,2048]{1,0:T(8,128)S(1)}, f32[64,2048]{1,0:T(8,128)S(1)}, u32[]{:S(2)}, u32[]{:S(2)}) collective-permute-start(f32[64,2048]{1,0:T(8,128)S(1)} %get-tuple-element.114), channel_id=1, source_target_pairs={{0,2},{1,3},{2,0},{3,1},{4,6},{5,7},{6,4},{7,5},{8,10},{9,11},{10,... | collective-permute-start | bytes 1572872 | tf_op jit(solution)/shard_map/ppermute | solution.py:338
  118.4 24.7 %collective-permute-start.23 = (f32[64,2048]{1,0:T(8,128)S(1)}, f32[64,2048]{1,0:T(8,128)S(1)}, u32[]{:S(2)}, u32[]{:S(2)}) collective-permute-start(f32[64,2048]{1,0:T(8,128)S(1)} %get-tuple-element.120), channel_id=1, source_target_pairs={{0,2},{1,3},{2,0},{3,1},{4,6},{5,7},{6,4},{7,5},{8,10},{9,11},{10,... | collective-permute-start | bytes 1572872 | tf_op jit(solution)/shard_map/ppermute | solution.py:338
  119.0 20.7 %collective-permute-start.22 = (bf16[8,64,256]{2,1,0:T(8,128)(2,1)S(1)}, bf16[8,64,256]{2,1,0:T(8,128)(2,1)S(1)}, u32[]{:S(2)}, u32[]{:S(2)}) collective-permute-start(bf16[8,64,256]{2,1,0:T(8,128)(2,1)S(1)} %join.4.own_ref), channel_id=1, source_target_pairs={{0,1},{1,0},{2,3},{3,2},{4,5},{5,4},{6,7},{7,6},{8,9},{9,8},{10,11... | collective-permute-start | bytes 786440 | tf_op jit(solution)/shard_map/ppermute | solution.py:338
  148.9 2.7 collective-permute-start.25
  149.0 4.1 %collective-permute-start.26 = (f32[128,2048]{1,0:T(8,128)S(1)}, f32[128,2048]{1,0:T(8,128)S(1)}, u32[]{:S(2)}, u32[]{:S(2)}) collective-permute-start(f32[128,2048]{1,0:T(8,128)S(1)} %get-tuple-element.126), channel_id=1, source_target_pairs={{0,1},{1,0},{2,3},{3,2},{4,5},{5,4},{6,7},{7,6},{8,9},{9,8},{10,11... | collective-permute-start | bytes 3145736 | tf_op jit(solution)/shard_map/ppermute | solution.py:338
  149.5 26.0 %collective-permute-start.28 = (bf16[64,2048]{1,0:T(8,128)(2,1)S(1)}, bf16[64,2048]{1,0:T(8,128)(2,1)S(1)}, u32[]{:S(2)}, u32[]{:S(2)}) collective-permute-start(bf16[64,2048]{1,0:T(8,128)(2,1)S(1)} %attention.6.refs_0_), channel_id=1, source_target_pairs={{0,2},{1,3},{2,0},{3,1},{4,6},{5,7},{6,4},{7,5},{8,10},{9,11},{10,... | collective-permute-start | bytes 786440 | tf_op jit(solution)/shard_map/ppermute | solution.py:338
  150.0 26.1 %collective-permute-start.29 = (bf16[64,2048]{1,0:T(8,128)(2,1)S(1)}, bf16[64,2048]{1,0:T(8,128)(2,1)S(1)}, u32[]{:S(2)}, u32[]{:S(2)}) collective-permute-start(bf16[64,2048]{1,0:T(8,128)(2,1)S(1)} %attention.6.refs_0_), channel_id=1, source_target_pairs={{0,1},{1,0},{2,3},{3,2},{4,5},{5,4},{6,7},{7,6},{8,9},{9,8},{10,11... | collective-permute-start | bytes 786440 | tf_op jit(solution)/shard_map/ppermute | solution.py:338
  150.0 27.7 %collective-permute-start.30 = (bf16[64,2048]{1,0:T(8,128)(2,1)S(1)}, bf16[64,2048]{1,0:T(8,128)(2,1)S(1)}, u32[]{:S(2)}, u32[]{:S(2)}) collective-permute-start(bf16[64,2048]{1,0:T(8,128)(2,1)S(1)} %attention.6.refs_0_), channel_id=1, source_target_pairs={{0,3},{1,2},{2,1},{3,0},{4,7},{5,6},{6,5},{7,4},{8,11},{9,10},{10,... | collective-permute-start | bytes 786440 | tf_op jit(solution)/shard_map/ppermute | solution.py:338
  153.8 23.9 %slice-start = ((s8[16777216]{0:T(1024)(128)(4,1)}), s8[4194304]{0:T(1024)(128)(4,1)S(1)}, s32[]{:S(2)}) async-start(s8[16777216]{0:T(1024)(128)(4,1)} %bitcast.25), calls=%async_computation | async-start | bytes 8388608
  153.8 23.8 %slice-start.1 = ((s8[16777216]{0:T(1024)(128)(4,1)}), s8[4194304]{0:T(1024)(128)(4,1)S(1)}, s32[]{:S(2)}) async-start(s8[16777216]{0:T(1024)(128)(4,1)} %bitcast.25), calls=%async_computation.1 | async-start | bytes 8388608
  153.8 23.8 %slice-start.2 = ((s8[16777216]{0:T(1024)(128)(4,1)}), s8[4194304]{0:T(1024)(128)(4,1)S(1)}, s32[]{:S(2)}) async-start(s8[16777216]{0:T(1024)(128)(4,1)} %bitcast.25), calls=%async_computation.2 | async-start | bytes 8388608
  153.8 21.7 %collective-permute-start.27 = (f32[64,2048]{1,0:T(8,128)S(1)}, f32[64,2048]{1,0:T(8,128)S(1)}, u32[]{:S(2)}, u32[]{:S(2)}) collective-permute-start(f32[64,2048]{1,0:T(8,128)S(1)} %get-tuple-element.129), channel_id=1, source_target_pairs={{0,2},{1,3},{2,0},{3,1},{4,6},{5,7},{6,4},{7,5},{8,10},{9,11},{10,... | collective-permute-start | bytes 1572872 | tf_op jit(solution)/shard_map/ppermute | solution.py:338
  169.1 31.2 %collective-permute-start.32 = (bf16[64,2048]{1,0:T(8,128)(2,1)S(1)}, bf16[64,2048]{1,0:T(8,128)(2,1)S(1)}, u32[]{:S(2)}, u32[]{:S(2)}) collective-permute-start(bf16[64,2048]{1,0:T(8,128)(2,1)S(1)} %attention.7.refs_0_), channel_id=1, source_target_pairs={{0,2},{1,3},{2,0},{3,1},{4,6},{5,7},{6,4},{7,5},{8,10},{9,11},{10,... | collective-permute-start | bytes 786440 | tf_op jit(solution)/shard_map/ppermute | solution.py:338
  175.5 25.3 %collective-permute-start.33 = (bf16[64,2048]{1,0:T(8,128)(2,1)S(1)}, bf16[64,2048]{1,0:T(8,128)(2,1)S(1)}, u32[]{:S(2)}, u32[]{:S(2)}) collective-permute-start(bf16[64,2048]{1,0:T(8,128)(2,1)S(1)} %attention.7.refs_0_), channel_id=1, source_target_pairs={{0,1},{1,0},{2,3},{3,2},{4,5},{5,4},{6,7},{7,6},{8,9},{9,8},{10,11... | collective-permute-start | bytes 786440 | tf_op jit(solution)/shard_map/ppermute | solution.py:338
  175.5 25.3 %collective-permute-start.34 = (bf16[64,2048]{1,0:T(8,128)(2,1)S(1)}, bf16[64,2048]{1,0:T(8,128)(2,1)S(1)}, u32[]{:S(2)}, u32[]{:S(2)}) collective-permute-start(bf16[64,2048]{1,0:T(8,128)(2,1)S(1)} %attention.7.refs_0_), channel_id=1, source_target_pairs={{0,3},{1,2},{2,1},{3,0},{4,7},{5,6},{6,5},{7,4},{8,11},{9,10},{10,... | collective-permute-start | bytes 786440 | tf_op jit(solution)/shard_map/ppermute | solution.py:338
  176.1 34.2 %collective-permute-start.36 = (f32[64,2048]{1,0:T(8,128)S(1)}, f32[64,2048]{1,0:T(8,128)S(1)}, u32[]{:S(2)}, u32[]{:S(2)}) collective-permute-start(f32[64,2048]{1,0:T(8,128)S(1)} %get-tuple-element.138), channel_id=1, source_target_pairs={{0,2},{1,3},{2,0},{3,1},{4,6},{5,7},{6,4},{7,5},{8,10},{9,11},{10,... | collective-permute-start | bytes 1572872 | tf_op jit(solution)/shard_map/ppermute | solution.py:338
  184.4 24.9 %collective-permute-start.31 = (f16[128,4096]{1,0:T(8,128)(2,1)S(1)}, f16[128,4096]{1,0:T(8,128)(2,1)S(1)}, u32[]{:S(2)}, u32[]{:S(2)}) collective-permute-start(f16[128,4096]{1,0:T(8,128)(2,1)S(1)} %multiply_convert_fusion.3), channel_id=1, source_target_pairs={{0,4},{4,0},{8,12},{12,8},{16,20},{20,16},{24,28},{28,24},{1,5},{5... | collective-permute-start | bytes 3145736 | tf_op jit(solution)/shard_map/ppermute | solution.py:341
  200.2 33.3 %collective-permute-start.39 = (bf16[64,2048]{1,0:T(8,128)(2,1)S(1)}, bf16[64,2048]{1,0:T(8,128)(2,1)S(1)}, u32[]{:S(2)}, u32[]{:S(2)}) collective-permute-start(bf16[64,2048]{1,0:T(8,128)(2,1)S(1)} %attention.8.refs_0_), channel_id=1, source_target_pairs={{0,2},{1,3},{2,0},{3,1},{4,6},{5,7},{6,4},{7,5},{8,10},{9,11},{10,... | collective-permute-start | bytes 786440 | tf_op jit(solution)/shard_map/ppermute | solution.py:338
  200.8 34.5 %collective-permute-start.40 = (bf16[64,2048]{1,0:T(8,128)(2,1)S(1)}, bf16[64,2048]{1,0:T(8,128)(2,1)S(1)}, u32[]{:S(2)}, u32[]{:S(2)}) collective-permute-start(bf16[64,2048]{1,0:T(8,128)(2,1)S(1)} %attention.8.refs_0_), channel_id=1, source_target_pairs={{0,1},{1,0},{2,3},{3,2},{4,5},{5,4},{6,7},{7,6},{8,9},{9,8},{10,11... | collective-permute-start | bytes 786440 | tf_op jit(solution)/shard_map/ppermute | solution.py:338
  207.8 17.9 %collective-permute-start.35 = (f16[128,2048]{1,0:T(8,128)(2,1)S(1)}, f16[128,2048]{1,0:T(8,128)(2,1)S(1)}, u32[]{:S(2)}, u32[]{:S(2)}) collective-permute-start(f16[128,2048]{1,0:T(8,128)(2,1)S(1)} %get-tuple-element.164), channel_id=1, source_target_pairs={{0,4},{4,0},{8,12},{12,8},{16,20},{20,16},{24,28},{28,24},{1,5},{5... | collective-permute-start | bytes 1572872 | tf_op jit(solution)/shard_map/ppermute | solution.py:341
  209.3 24.1 %collective-permute-start.38 = (f16[128,2048]{1,0:T(8,128)(2,1)S(1)}, f16[128,2048]{1,0:T(8,128)(2,1)S(1)}, u32[]{:S(2)}, u32[]{:S(2)}) collective-permute-start(f16[128,2048]{1,0:T(8,128)(2,1)S(1)} %get-tuple-element.163), channel_id=1, source_target_pairs={{0,4},{4,0},{8,12},{12,8},{16,20},{20,16},{24,28},{28,24},{1,5},{5... | collective-permute-start | bytes 1572872 | tf_op jit(solution)/shard_map/ppermute | solution.py:341
  210.3 24.9 %collective-permute-start.41 = (bf16[64,2048]{1,0:T(8,128)(2,1)S(1)}, bf16[64,2048]{1,0:T(8,128)(2,1)S(1)}, u32[]{:S(2)}, u32[]{:S(2)}) collective-permute-start(bf16[64,2048]{1,0:T(8,128)(2,1)S(1)} %attention.8.refs_0_), channel_id=1, source_target_pairs={{0,3},{1,2},{2,1},{3,0},{4,7},{5,6},{6,5},{7,4},{8,11},{9,10},{10,... | collective-permute-start | bytes 786440 | tf_op jit(solution)/shard_map/ppermute | solution.py:338
  225.7 18.6 %collective-permute-start.47 = (bf16[64,2048]{1,0:T(8,128)(2,1)S(1)}, bf16[64,2048]{1,0:T(8,128)(2,1)S(1)}, u32[]{:S(2)}, u32[]{:S(2)}) collective-permute-start(bf16[64,2048]{1,0:T(8,128)(2,1)S(1)} %attention.9.refs_0_), channel_id=1, source_target_pairs={{0,2},{1,3},{2,0},{3,1},{4,6},{5,7},{6,4},{7,5},{8,10},{9,11},{10,... | collective-permute-start | bytes 786440 | tf_op jit(solution)/shard_map/ppermute | solution.py:338
  233.4 10.9 %collective-permute-start.48 = (bf16[64,2048]{1,0:T(8,128)(2,1)S(1)}, bf16[64,2048]{1,0:T(8,128)(2,1)S(1)}, u32[]{:S(2)}, u32[]{:S(2)}) collective-permute-start(bf16[64,2048]{1,0:T(8,128)(2,1)S(1)} %attention.9.refs_0_), channel_id=1, source_target_pairs={{0,1},{1,0},{2,3},{3,2},{4,5},{5,4},{6,7},{7,6},{8,9},{9,8},{10,11... | collective-permute-start | bytes 786440 | tf_op jit(solution)/shard_map/ppermute | solution.py:338
  233.6 10.7 %collective-permute-start.49 = (bf16[64,2048]{1,0:T(8,128)(2,1)S(1)}, bf16[64,2048]{1,0:T(8,128)(2,1)S(1)}, u32[]{:S(2)}, u32[]{:S(2)}) collective-permute-start(bf16[64,2048]{1,0:T(8,128)(2,1)S(1)} %attention.9.refs_0_), channel_id=1, source_target_pairs={{0,3},{1,2},{2,1},{3,0},{4,7},{5,6},{6,5},{7,4},{8,11},{9,10},{10,... | collective-permute-start | bytes 786440 | tf_op jit(solution)/shard_map/ppermute | solution.py:338
  242.2 14.9 %collective-permute-start.42 = (f16[128,2048]{1,0:T(8,128)(2,1)S(1)}, f16[128,2048]{1,0:T(8,128)(2,1)S(1)}, u32[]{:S(2)}, u32[]{:S(2)}) collective-permute-start(f16[128,2048]{1,0:T(8,128)(2,1)S(1)} %get-tuple-element.162), channel_id=1, source_target_pairs={{0,4},{4,0},{8,12},{12,8},{16,20},{20,16},{24,28},{28,24},{1,5},{5... | collective-permute-start | bytes 1572872 | tf_op jit(solution)/shard_map/ppermute | solution.py:341
  243.2 25.1 %collective-permute-start.44 = (f16[128,2048]{1,0:T(8,128)(2,1)S(1)}, f16[128,2048]{1,0:T(8,128)(2,1)S(1)}, u32[]{:S(2)}, u32[]{:S(2)}) collective-permute-start(f16[128,2048]{1,0:T(8,128)(2,1)S(1)} %get-tuple-element.161), channel_id=1, source_target_pairs={{0,4},{4,0},{8,12},{12,8},{16,20},{20,16},{24,28},{28,24},{1,5},{5... | collective-permute-start | bytes 1572872 | tf_op jit(solution)/shard_map/ppermute | solution.py:341
  257.2 12.6 %collective-permute-start.43 = (f16[128,2048]{1,0:T(8,128)(2,1)S(1)}, f16[128,2048]{1,0:T(8,128)(2,1)S(1)}, u32[]{:S(2)}, u32[]{:S(2)}) collective-permute-start(f16[128,2048]{1,0:T(8,128)(2,1)S(1)} %add_convert_fusion.7), channel_id=1, source_target_pairs={{0,8},{4,12},{24,16},{28,20},{1,9},{5,13},{25,17},{29,21},{2,10},{... | collective-permute-start | bytes 1572872 | tf_op jit(solution)/shard_map/ppermute | solution.py:345
  258.8 20.7 %collective-permute-start.50 = (f16[128,2048]{1,0:T(8,128)(2,1)S(1)}, f16[128,2048]{1,0:T(8,128)(2,1)S(1)}, u32[]{:S(2)}, u32[]{:S(2)}) collective-permute-start(f16[128,2048]{1,0:T(8,128)(2,1)S(1)} %get-tuple-element.159), channel_id=1, source_target_pairs={{0,4},{4,0},{8,12},{12,8},{16,20},{20,16},{24,28},{28,24},{1,5},{5... | collective-permute-start | bytes 1572872 | tf_op jit(solution)/shard_map/ppermute | solution.py:341
  260.3 29.5 %collective-permute-start.53 = (f16[128,2048]{1,0:T(8,128)(2,1)S(1)}, f16[128,2048]{1,0:T(8,128)(2,1)S(1)}, u32[]{:S(2)}, u32[]{:S(2)}) collective-permute-start(f16[128,2048]{1,0:T(8,128)(2,1)S(1)} %get-tuple-element.160), channel_id=1, source_target_pairs={{0,4},{4,0},{8,12},{12,8},{16,20},{20,16},{24,28},{28,24},{1,5},{5... | collective-permute-start | bytes 1572872 | tf_op jit(solution)/shard_map/ppermute | solution.py:341
  268.4 12.6 %collective-permute-start.46 = (f16[128,2048]{1,0:T(8,128)(2,1)S(1)}, f16[128,2048]{1,0:T(8,128)(2,1)S(1)}, u32[]{:S(2)}, u32[]{:S(2)}) collective-permute-start(f16[128,2048]{1,0:T(8,128)(2,1)S(1)} %add_convert_fusion.6), channel_id=1, source_target_pairs={{0,8},{4,12},{24,16},{28,20},{1,9},{5,13},{25,17},{29,21},{2,10},{... | collective-permute-start | bytes 1572872 | tf_op jit(solution)/shard_map/ppermute | solution.py:345
  270.1 11.9 %collective-permute-start.45 = (f16[128,2048]{1,0:T(8,128)(2,1)S(1)}, f16[128,2048]{1,0:T(8,128)(2,1)S(1)}, u32[]{:S(2)}, u32[]{:S(2)}) collective-permute-start(f16[128,2048]{1,0:T(8,128)(2,1)S(1)} %add_convert_fusion.5), channel_id=1, source_target_pairs={{8,16},{12,20},{16,8},{20,12},{9,17},{13,21},{17,9},{21,13},{10,18... | collective-permute-start | bytes 1572872 | tf_op jit(solution)/shard_map/ppermute | solution.py:345
  279.7 13.7 %collective-permute-start.52 = (f16[128,2048]{1,0:T(8,128)(2,1)S(1)}, f16[128,2048]{1,0:T(8,128)(2,1)S(1)}, u32[]{:S(2)}, u32[]{:S(2)}) collective-permute-start(f16[128,2048]{1,0:T(8,128)(2,1)S(1)} %add_convert_fusion.4), channel_id=1, source_target_pairs={{0,8},{4,12},{24,16},{28,20},{1,9},{5,13},{25,17},{29,21},{2,10},{... | collective-permute-start | bytes 1572872 | tf_op jit(solution)/shard_map/ppermute | solution.py:345
  281.3 13.6 %collective-permute-start.56 = (f16[128,2048]{1,0:T(8,128)(2,1)S(1)}, f16[128,2048]{1,0:T(8,128)(2,1)S(1)}, u32[]{:S(2)}, u32[]{:S(2)}) collective-permute-start(f16[128,2048]{1,0:T(8,128)(2,1)S(1)} %add_convert_fusion.3), channel_id=1, source_target_pairs={{8,16},{12,20},{16,8},{20,12},{9,17},{13,21},{17,9},{21,13},{10,18... | collective-permute-start | bytes 1572872 | tf_op jit(solution)/shard_map/ppermute | solution.py:345
  289.9 13.7 %collective-permute-start.58 = (f16[128,2048]{1,0:T(8,128)(2,1)S(1)}, f16[128,2048]{1,0:T(8,128)(2,1)S(1)}, u32[]{:S(2)}, u32[]{:S(2)}) collective-permute-start(f16[128,2048]{1,0:T(8,128)(2,1)S(1)} %add_convert_fusion.2), channel_id=1, source_target_pairs={{0,8},{4,12},{24,16},{28,20},{1,9},{5,13},{25,17},{29,21},{2,10},{... | collective-permute-start | bytes 1572872 | tf_op jit(solution)/shard_map/ppermute | solution.py:345
  291.3 23.6 %collective-permute-start.55 = (f16[128,2048]{1,0:T(8,128)(2,1)S(1)}, f16[128,2048]{1,0:T(8,128)(2,1)S(1)}, u32[]{:S(2)}, u32[]{:S(2)}) collective-permute-start(f16[128,2048]{1,0:T(8,128)(2,1)S(1)} %add_convert_fusion.8), channel_id=1, source_target_pairs={{8,0},{12,4},{16,24},{20,28},{0,8},{4,12},{24,16},{28,20},{9,1},{1... | collective-permute-start | bytes 1572872 | tf_op jit(solution)/shard_map/ppermute | solution.py:345
  291.4 33.1 %collective-permute-start.37 = (f16[128,2048]{1,0:T(8,128)(2,1)S(1)}, f16[128,2048]{1,0:T(8,128)(2,1)S(1)}, u32[]{:S(2)}, u32[]{:S(2)}) collective-permute-start(f16[128,2048]{1,0:T(8,128)(2,1)S(1)} %add_convert_fusion.9), channel_id=1, source_target_pairs={{8,0},{12,4},{16,24},{20,28},{0,8},{4,12},{24,16},{28,20},{9,1},{1... | collective-permute-start | bytes 1572872 | tf_op jit(solution)/shard_map/ppermute | solution.py:345
  293.4 44.6 %collective-permute-start.51 = (f16[128,2048]{1,0:T(8,128)(2,1)S(1)}, f16[128,2048]{1,0:T(8,128)(2,1)S(1)}, u32[]{:S(2)}, u32[]{:S(2)}) collective-permute-start(f16[128,2048]{1,0:T(8,128)(2,1)S(1)} %collective-permute-done.45), channel_id=1, source_target_pairs={{8,0},{12,4},{16,24},{20,28},{9,1},{13,5},{17,25},{21,29},{10,2},{... | collective-permute-start | bytes 1572872 | tf_op jit(solution)/shard_map/ppermute | solution.py:345
  295.0 43.1 %collective-permute-start.54 = (f16[128,2048]{1,0:T(8,128)(2,1)S(1)}, f16[128,2048]{1,0:T(8,128)(2,1)S(1)}, u32[]{:S(2)}, u32[]{:S(2)}) collective-permute-start(f16[128,2048]{1,0:T(8,128)(2,1)S(1)} %add_convert_fusion.1), channel_id=1, source_target_pairs={{8,16},{12,20},{16,8},{20,12},{9,17},{13,21},{17,9},{21,13},{10,18... | collective-permute-start | bytes 1572872 | tf_op jit(solution)/shard_map/ppermute | solution.py:345
  303.6 34.4 %collective-permute-start.57 = (f16[128,2048]{1,0:T(8,128)(2,1)S(1)}, f16[128,2048]{1,0:T(8,128)(2,1)S(1)}, u32[]{:S(2)}, u32[]{:S(2)}) collective-permute-start(f16[128,2048]{1,0:T(8,128)(2,1)S(1)} %collective-permute-done.56), channel_id=1, source_target_pairs={{8,0},{12,4},{16,24},{20,28},{9,1},{13,5},{17,25},{21,29},{10,2},{... | collective-permute-start | bytes 1572872 | tf_op jit(solution)/shard_map/ppermute | solution.py:345
  314.9 23.2 %collective-permute-start.59 = (f16[128,2048]{1,0:T(8,128)(2,1)S(1)}, f16[128,2048]{1,0:T(8,128)(2,1)S(1)}, u32[]{:S(2)}, u32[]{:S(2)}) collective-permute-start(f16[128,2048]{1,0:T(8,128)(2,1)S(1)} %add_convert_fusion), channel_id=1, source_target_pairs={{8,16},{12,20},{16,8},{20,12},{9,17},{13,21},{17,9},{21,13},{10,18... | collective-permute-start | bytes 1572872 | tf_op jit(solution)/shard_map/ppermute | solution.py:345
  (12 other events, 85.5 us)
